TPU v7x, 32 devices: a whole 2x2x4 slice. The times are simulated.
32 devices in a mesh: dp: 4 (over z), section: 4 (over x, core), mp: 2 (over y).
Axes of the slice: x: 2, y: 2, z: 4, core: 2. Of those that a mesh axis runs over, the one named last changes fastest.
Arguments:
- act_in: bfloat16 [4, 1024, 4096], P('section', 'dp', 'mp'), may hold values from -6 to 6
- weights: bfloat16 [4, 4096, 4096], P('section', None, 'mp'), may hold values from -0.09375 to 0.09375
- act_saved: bfloat16 [4, 1024, 4096], P('section', 'dp', 'mp'), may hold values from -6 to 6
- cotangent: bfloat16 [4, 1024, 4096], P('section', 'dp', 'mp'), may hold values from -6 to 6
Outputs:
- received: bfloat16 [4, 1024, 4096], P('section', 'dp', 'mp')
- shadow: bfloat16 [4, 1024, 4096], P('section', 'dp', 'mp')
- grad_back: bfloat16 [4, 1024, 4096], P('section', 'dp', 'mp')
- weight_grad: bfloat16 [4, 4096, 4096], P('section', 'dp', 'mp')
All inputs are finite; a program needn't handle non-finite values.
Results may differ from a plain program's by a relative error of at most 0.009.
Values may be sent and summed in bfloat16 or wider, within the bound.
No kernel may reach another device: no remote copies, remote signals or barrier semaphores. Data moves between devices by JAX's collectives and lax.ppermute only.
A program may use at most 192 MiB of HBM per device.

v0:
```python
import jax
import jax.numpy as jnp
from jax import lax
from jax.sharding import PartitionSpec as P

EPS = 1e-05


def from_behind(value, axis, steps):
    count = lax.axis_size(axis)
    pairs = [(source, (source + steps) % count) for source in range(count)]
    return lax.ppermute(value, axis, pairs)


def normalize(rows):
    values = rows.astype(jnp.float32)
    average = jnp.mean(values, axis=-1, keepdims=True)
    centred = values - average
    spread = jnp.mean(centred * centred, axis=-1, keepdims=True)
    inverse = lax.rsqrt(spread + EPS)
    return (centred * inverse, inverse)


def forward_layer(full_rows, own_rows, weight):
    scaled, inverse = normalize(full_rows)
    normed = scaled.astype(jnp.bfloat16)
    preact = jnp.dot(normed, weight, preferred_element_type=jnp.float32)
    return (own_rows.astype(jnp.float32) + jax.nn.gelu(preact)).astype(jnp.bfloat16)


def body(act_in, weights, act_saved, cotangent):
    weight = weights[0]
    own_in = act_in[0]
    own_cot = cotangent[0]
    columns = weight.shape[1]
    col_start = lax.axis_index("mp") * columns
    full_in, full_saved = (
        lax.all_gather(own_in, "mp", axis=1, tiled=True),
        lax.all_gather(act_saved[0], "mp", axis=1, tiled=True),
    )
    forward = forward_layer(full_in, own_in, weight)
    received = from_behind(forward, "section", 1)
    next_weight = from_behind(weight, "section", -1)
    forward_full = lax.all_gather(forward, "mp", axis=1, tiled=True)
    shadow = forward_layer(forward_full, forward, next_weight)
    scaled, inverse = normalize(full_saved)
    normed = scaled.astype(jnp.bfloat16)
    preact = jnp.dot(normed, weight, preferred_element_type=jnp.float32)
    _, pullback = jax.vjp(jax.nn.gelu, preact)
    pre_grad = pullback(own_cot.astype(jnp.float32))[0].astype(jnp.bfloat16)
    weight_grad = lax.psum_scatter(
        lax.dot_general(
            normed, pre_grad, (((0,), (0,)), ((), ())), preferred_element_type=jnp.float32
        ).astype(jnp.bfloat16),
        "dp",
        scatter_dimension=0,
        tiled=True,
    )
    dnormed_part = lax.dot_general(
        pre_grad, weight, (((1,), (1,)), ((), ())), preferred_element_type=jnp.float32
    )
    scaled_own = lax.dynamic_slice_in_dim(scaled, col_start, columns, 1)
    dnormed = lax.psum(dnormed_part, "mp")
    first = jnp.mean(dnormed, axis=-1, keepdims=True)
    second = jnp.mean(dnormed * scaled, axis=-1, keepdims=True)
    dnormed_own = lax.dynamic_slice_in_dim(dnormed, col_start, columns, 1)
    input_grad = own_cot.astype(jnp.float32) + inverse * (dnormed_own - first - scaled_own * second)
    grad_back = from_behind(input_grad.astype(jnp.bfloat16), "section", -1)
    return (received[None], shadow[None], grad_back[None], weight_grad[None])


def solution(mesh):
    return jax.shard_map(
        body,
        mesh=mesh,
        in_specs=(
            P("section", "dp", "mp"),
            P("section", None, "mp"),
            P("section", "dp", "mp"),
            P("section", "dp", "mp"),
        ),
        out_specs=(
            P("section", "dp", "mp"),
            P("section", "dp", "mp"),
            P("section", "dp", "mp"),
            P("section", "dp", "mp"),
        ),
        check_vma=False,
    )
```

profile of v0, /device:TPU:8, one launch (start us, length us, event | category | flops | bytes accessed | tf_op | source)
XLA Modules:
  0.0 514.0 jit_solution(8068618785782070238)
XLA Ops:
  7.2 0.7 all-gather.10.cloned.1.call-update
  7.9 0.7 all-gather.8.cloned.1.call-update
  8.7 35.2 %all-gather.10.cloned.1.call-done = bf16[1,256,4096]{2,1,0:T(8,128)(2,1)} async-done(((bf16[1,256,2048]{2,1,0:T(8,128)(2,1)}), bf16[1,256,4096]{2,1,0:T(8,128)(2,1)}) %all-gather.10.cloned.1.call-update) | async-done | bytes 2097168 | tf_op jit(solution)/shard_map/all_gather | solution.py:39
  43.9 2.1 convert_reduce_fusion
  46.1 0.7 fusion.12
  46.8 9.9 %fusion.67 = f32[256,2048]{1,0:T(8,128)} fusion(bf16[1,4096,2048]{2,1,0:T(8,128)(2,1)} %param.5, bf16[1,256,4096]{2,1,0:T(8,128)(2,1)S(1)} %copy-done, f32[256]{0:T(256)S(1)} %add_rsqrt_fusion, f32[256]{0:T(256)S(1)} %broadcast_multiply_fusion.2), kind=kOutput, calls=%fused_computation.72 | convolution fusion | flops 4299161600 | bytes 20973568 | tf_op jit(solution)/shard_map/dot_general | solution.py:48
  56.7 13.9 %fusion.54 = f32[256,4096]{1,0:T(8,128)} fusion(f32[256,2048]{1,0:T(8,128)} %fusion.67, bf16[1,256,2048]{2,1,0:T(8,128)(2,1)S(1)} %copy-done.4, bf16[1,4096,2048]{2,1,0:T(8,128)(2,1)} %param.5), kind=kOutput, calls=%fused_computation.60 | convolution fusion | flops 4305977344 | bytes 24117248 | tf_op jit(solution)/shard_map/dot_general | solution.py:59
  70.9 7.7 %all-gather.8.cloned.1.call-done = bf16[1,256,4096]{2,1,0:T(8,128)(2,1)} async-done(((bf16[1,256,2048]{2,1,0:T(8,128)(2,1)}), bf16[1,256,4096]{2,1,0:T(8,128)(2,1)}) %all-gather.8.cloned.1.call-update) | async-done | bytes 2097168 | tf_op jit(solution)/shard_map/all_gather | solution.py:38
  78.6 2.1 convert_reduce_fusion.1
  80.8 0.7 fusion.7
  81.5 12.3 %fusion.28 = bf16[256,2048]{1,0:T(8,128)(2,1)} fusion(bf16[1,256,4096]{2,1,0:T(8,128)(2,1)S(1)} %copy-done.3, f32[256]{0:T(256)S(1)} %add_rsqrt_fusion.2, f32[256]{0:T(256)S(1)} %broadcast_multiply_fusion.4, bf16[1,256,2048]{2,1,0:T(8,128)(2,1)S(1)} %copy-done.5, bf16[1,4096,2048]{2,1,0:T(8,128)(2,1)} %param.5), kind=kOutput, calls=%fused_computation.43 | convolution fusion | flops 4304928768 | bytes 20973568 | tf_op jit(solution)/shard_map/dot_general | solution.py:27
  93.9 11.0 %convolution_convert_fusion = bf16[4096,2048]{1,0:T(8,128)(2,1)} fusion(f32[256,2048]{1,0:T(8,128)} %fusion.67, bf16[1,256,2048]{2,1,0:T(8,128)(2,1)S(1)} %copy-done.4, bf16[1,256,4096]{2,1,0:T(8,128)(2,1)S(1)} %copy-done, f32[256]{0:T(256)S(1)} %add_rsqrt_fusion, f32[256]{0:T(256)S(1)} %broadcast_multiply_fusion.2), kind=kOutput, calls=%fused_computation | convolution fusion | flops 4318560256 | bytes 22022144 | tf_op jit(solution)/shard_map/dot_general | solution.py:52
  105.5 83.4 %all-reduce.2.cloned.1.call-done = f32[256,4096]{1,0:T(8,128)} async-done(((f32[256,4096]{1,0:T(8,128)}), f32[256,4096]{1,0:T(8,128)}) %all-reduce.2.cloned.1.call-update) | async-done | bytes 4194320 | tf_op jit(solution)/shard_map/psum | solution.py:63
  188.9 3.3 fusion.94
  192.4 1.6 fusion.41
  193.9 0.9 collective-permute-start.2
  194.8 29.3 %all-gather.6.cloned.1.call-done = bf16[256,4096]{1,0:T(8,128)(2,1)} async-done(((bf16[256,2048]{1,0:T(8,128)(2,1)}), bf16[256,4096]{1,0:T(8,128)(2,1)}) %all-gather.6.cloned.1.call-update) | async-done | bytes 2097168 | tf_op jit(solution)/shard_map/all_gather | solution.py:44
  224.1 2.1 convert_reduce_fusion.2
  226.3 0.7 fusion.2
  227.0 82.1 %collective-permute-done.2 = bf16[256,2048]{1,0:T(8,128)(2,1)S(1)} collective-permute-done((bf16[256,2048]{1,0:T(8,128)(2,1)}, bf16[256,2048]{1,0:T(8,128)(2,1)S(1)}, u32[]{:S(2)}, u32[]{:S(2)}) %collective-permute-start.2) | collective-permute-done | bytes 1048608 | tf_op jit(solution)/shard_map/ppermute | solution.py:12
  309.1 11.9 %fusion.50 = bf16[1,256,2048]{2,1,0:T(8,128)(2,1)} fusion(bf16[4096,2048]{1,0:T(8,128)(2,1)} %collective-permute-done.1, bf16[256,4096]{1,0:T(8,128)(2,1)S(1)} %copy-done.2, f32[256]{0:T(256)S(1)} %add_rsqrt_fusion.1, f32[256]{0:T(256)S(1)} %broadcast_multiply_fusion.3, bf16[256,2048]{1,0:T(8,128)(2,1)S(1)} %copy-done.6), kind=kOutput, calls=%fused_computation.59 | convolution fusion | flops 4304928768 | bytes 20973568 | tf_op jit(solution)/shard_map/dot_general | solution.py:27
  321.0 183.1 %reduce-scatter.2.cloned.1.call-done = bf16[1024,2048]{1,0:T(8,128)(2,1)} async-done(((bf16[4096,2048]{1,0:T(8,128)(2,1)}), bf16[1024,2048]{1,0:T(8,128)(2,1)}) %reduce-scatter.2.cloned.1.call-update) | async-done | bytes 4194320 | tf_op jit(solution)/shard_map/reduce_scatter | solution.py:51
  504.2 2.3 copy.11
  506.5 1.0 copy.12
  (33 shorter events, 1.6 us)
Async XLA Ops:
  7.2 36.7 %all-gather.10.cloned.1.call-start = ((), (), s32[]{:S(2)}) async-start(), calls=%async_computation.5 | async-start | bytes 3145728 | tf_op jit(solution)/shard_map/all_gather | solution.py:39
  7.9 70.7 %all-gather.8.cloned.1.call-start = ((), (), s32[]{:S(2)}) async-start(), calls=%async_computation.4 | async-start | bytes 3145728 | tf_op jit(solution)/shard_map/all_gather | solution.py:38
  8.6 180.3 %all-reduce.2.cloned.1.call-start = ((), (), s32[]{:S(2)}) async-start(), calls=%async_computation.2 | async-start | bytes 8388608 | tf_op jit(solution)/shard_map/psum | solution.py:63
  43.9 2.2 copy-start
  46.8 9.9 %copy-start.4 = (bf16[1,256,2048]{2,1,0:T(8,128)(2,1)S(1)}, bf16[1,256,2048]{2,1,0:T(8,128)(2,1)}, u32[]{:S(2)}) copy-start(bf16[1,256,2048]{2,1,0:T(8,128)(2,1)} %param.7) | copy-start | bytes 3145732
  70.6 153.5 %all-gather.6.cloned.1.call-start = ((), (), s32[]{:S(2)}) async-start(), calls=%async_computation.1 | async-start | bytes 3145728 | tf_op jit(solution)/shard_map/all_gather | solution.py:44
  78.6 2.2 copy-start.3
  78.6 2.9 copy-start.5
  93.8 410.3 %reduce-scatter.2.cloned.1.call-start = ((), (), s32[]{:S(2)}) async-start(), calls=%async_computation.3 | async-start | bytes 20971520 | tf_op jit(solution)/shard_map/reduce_scatter | solution.py:51
  104.9 204.2 %collective-permute-start.1 = (bf16[4096,2048]{1,0:T(8,128)(2,1)}, bf16[4096,2048]{1,0:T(8,128)(2,1)}, u32[]{:S(2)}, u32[]{:S(2)}) collective-permute-start(bf16[4096,2048]{1,0:T(8,128)(2,1)} %bitcast.61), channel_id=1, source_target_pairs={{0,6},{2,0},{4,2},{6,4},{1,7},{3,1},{5,3},{7,5},{8,14},{10,8},{12,... | collective-permute-start | bytes 50331656 | tf_op jit(solution)/shard_map/ppermute | solution.py:12
  105.5 89.3 %collective-permute-start = (bf16[256,2048]{1,0:T(8,128)(2,1)}, bf16[256,2048]{1,0:T(8,128)(2,1)}, u32[]{:S(2)}, u32[]{:S(2)}) collective-permute-start(bf16[256,2048]{1,0:T(8,128)(2,1)} %fusion.28), channel_id=1, source_target_pairs={{0,2},{2,4},{4,6},{6,0},{1,3},{3,5},{5,7},{7,1},{8,10},{10,12},{12... | collective-permute-start | bytes 3145736 | tf_op jit(solution)/shard_map/ppermute | solution.py:12
  188.9 3.4 copy-start.1
  193.9 115.2 %collective-permute-start.2 = (bf16[256,2048]{1,0:T(8,128)(2,1)}, bf16[256,2048]{1,0:T(8,128)(2,1)S(1)}, u32[]{:S(2)}, u32[]{:S(2)}) collective-permute-start(bf16[256,2048]{1,0:T(8,128)(2,1)} %fusion.41), channel_id=1, source_target_pairs={{0,6},{2,0},{4,2},{6,4},{1,7},{3,1},{5,3},{7,5},{8,14},{10,8},{12,... | collective-permute-start | bytes 3145736 | tf_op jit(solution)/shard_map/ppermute | solution.py:12
  224.1 2.2 copy-start.2
  224.1 85.0 %copy-start.6 = (bf16[256,2048]{1,0:T(8,128)(2,1)S(1)}, bf16[256,2048]{1,0:T(8,128)(2,1)}, u32[]{:S(2)}) copy-start(bf16[256,2048]{1,0:T(8,128)(2,1)} %fusion.28) | copy-start | bytes 3145732
Sparse Core Ops, SparseCore 0:
  9.5 34.2 all-gather.9
  45.4 33.1 all-gather.7
  81.0 107.8 all-reduce.1
  191.0 33.1 all-gather.5
  227.0 277.1 reduce-scatter.1
where the time goes:
time: 519 us; the launch traced here: 514 us
  waiting for transfers between devices  422 us (81%)
  matrix products  59 us (11%)
  between operations  13.8 us (3%)
  other arithmetic  13.3 us (3%)
    reduce_scatter x1, waiting for transfers between devices, body(): lax.psum_scatter(lax.dot_general(normed, pre_grad, (((0,), (0,)), ((), ()...  183 us
    psum x1, waiting for transfers between devices, body(): dnormed = lax.psum(dnormed_part, 'mp')  83.4 us
    ppermute x3, waiting for transfers between devices, from_behind(): return lax.ppermute(value, axis, pairs)  82.1 us
    all_gather x1, waiting for transfers between devices, body(): lax.all_gather(act_saved[0], 'mp', axis=1, tiled=True)  35.2 us
    all_gather x1, waiting for transfers between devices, body(): forward_full = lax.all_gather(forward, 'mp', axis=1, tiled=True)  29.3 us
    dot_general x2, matrix products, forward_layer(): preact = jnp.dot(normed, weight, preferred_element_type=jnp.float32)  24.2 us
    dot_general x1, matrix products, body(): lax.dot_general(pre_grad, weight, (((1,), (1,)), ((), ())), preferred_ele...  13.9 us
    dot_general x1, matrix products, body(): lax.dot_general(normed, pre_grad, (((0,), (0,)), ((), ())), preferred_ele...  11 us
  transfers between devices with their start and end apart: 8, of which 6 were waited for; matrix products, arithmetic and copies ran while one was open for 14% of the time, Pallas kernels for 0%

commit v1 on v0

v1 whole, which is shorter than its diff:
```python
import jax
import jax.numpy as jnp
from jax import lax
from jax.sharding import PartitionSpec as P

EPS = 1e-05


def shift(value, axis, steps):
    count = lax.axis_size(axis)
    return lax.ppermute(value, axis, [(at, (at + steps) % count) for at in range(count)])


def swap(value, axis):
    return shift(value, axis, 1)


def line(value, axis, steps):
    count = lax.axis_size(axis)
    pairs = [(at, at + steps) for at in range(count) if 0 <= at + steps < count]
    return lax.ppermute(value, axis, pairs)


def shift_and_swap(value, steps):
    sections, halves = lax.axis_size("section"), lax.axis_size("mp")
    pairs = [
        (at * halves + half, ((at + steps) % sections) * halves + (half + 1) % halves)
        for at in range(sections)
        for half in range(halves)
    ]
    return lax.ppermute(value, ("section", "mp"), pairs)


def whole_rows(own, other):
    first = lax.axis_index("mp") == 0
    return jnp.concatenate([jnp.where(first, own, other), jnp.where(first, other, own)], axis=1)


def normalize(rows):
    values = rows.astype(jnp.float32)
    average = jnp.mean(values, axis=-1, keepdims=True)
    centred = values - average
    spread = jnp.mean(centred * centred, axis=-1, keepdims=True)
    inverse = lax.rsqrt(spread + EPS)
    return (centred * inverse, inverse)


def forward_layer(full_rows, own_rows, weight):
    normed = normalize(full_rows)[0].astype(jnp.bfloat16)
    preact = jnp.dot(normed, weight, preferred_element_type=jnp.float32)
    return (own_rows.astype(jnp.float32) + jax.nn.gelu(preact)).astype(jnp.bfloat16)


def body(act_in, weights, act_saved, cotangent):
    weight = weights[0]
    own_in, own_saved, own_cot = act_in[0], act_saved[0], cotangent[0]
    depth, columns = weight.shape
    replicas = lax.axis_size("dp")
    me_dp, me_mp = lax.axis_index("dp"), lax.axis_index("mp")
    own_at, other_at = me_mp * columns, (1 - me_mp) * columns
    block = depth // replicas

    other_saved = swap(own_saved, "mp")
    other_in = swap(own_in, "mp")

    scaled, inverse = normalize(whole_rows(own_saved, other_saved))
    normed = scaled.astype(jnp.bfloat16)
    normed_blocks = [lax.dynamic_slice_in_dim(normed, me_dp * block, block, 1)]
    for steps in range(1, replicas):
        target = (me_dp + steps) % replicas
        normed_blocks.append(
            shift(lax.dynamic_slice_in_dim(normed, target * block, block, 1), "dp", steps)
        )
    preact = jnp.dot(normed, weight, preferred_element_type=jnp.float32)
    _, pullback = jax.vjp(jax.nn.gelu, preact)
    pre_grad = pullback(own_cot.astype(jnp.float32))[0].astype(jnp.bfloat16)

    ups, downs = [pre_grad], [pre_grad]
    for _ in range(1, replicas):
        ups.append(line(ups[-1], "dp", 1))
        downs.append(line(downs[-1], "dp", -1))
    grads = [pre_grad] + [
        jnp.where(me_dp >= steps, ups[steps], downs[replicas - steps])
        for steps in range(1, replicas)
    ]

    part = lax.dot_general(
        pre_grad, weight, (((1,), (1,)), ((), ())), preferred_element_type=jnp.float32
    )
    sums = jnp.stack([jnp.sum(part, axis=-1), jnp.sum(part * scaled, axis=-1)])
    part_other = lax.dynamic_slice_in_dim(part, other_at, columns, 1).astype(jnp.bfloat16)
    part_own = lax.dynamic_slice_in_dim(part, own_at, columns, 1)
    sums = (sums + swap(sums, "mp")) / depth
    dnormed = part_own + swap(part_other, "mp").astype(jnp.float32)
    scaled_own = lax.dynamic_slice_in_dim(scaled, own_at, columns, 1)
    input_grad = own_cot.astype(jnp.float32) + inverse * (
        dnormed - sums[0][:, None] - scaled_own * sums[1][:, None]
    )
    grad_back = shift(input_grad.astype(jnp.bfloat16), "section", -1)

    forward = forward_layer(whole_rows(own_in, other_in), own_in, weight)
    received = shift(forward, "section", 1)
    received_other = shift_and_swap(forward, 1)
    shadow_there = forward_layer(whole_rows(received, received_other), received, weight)
    shadow = shift(shadow_there, "section", -1)

    weight_grad = lax.dot_general(
        jnp.concatenate(normed_blocks, axis=0),
        jnp.concatenate(grads, axis=0),
        (((0,), (0,)), ((), ())),
        preferred_element_type=jnp.float32,
    ).astype(jnp.bfloat16)
    return (received[None], shadow[None], grad_back[None], weight_grad[None])


def solution(mesh):
    return jax.shard_map(
        body,
        mesh=mesh,
        in_specs=(
            P("section", "dp", "mp"),
            P("section", None, "mp"),
            P("section", "dp", "mp"),
            P("section", "dp", "mp"),
        ),
        out_specs=(
            P("section", "dp", "mp"),
            P("section", "dp", "mp"),
            P("section", "dp", "mp"),
            P("section", "dp", "mp"),
        ),
        check_vma=False,
    )
```

time: 519 us -> 281 us (0.54)
  waiting for transfers between devices: 422 us -> 169 us
  starting transfers between devices: 1.9 us -> 32.2 us
  between operations: 13.8 us -> 0.92 us
  matrix products: 59 us -> 52.8 us
  local copies, waits for them, and re-layouts: 3.75 us -> 9.92 us
    reduce_scatter x1 -> x0, waiting for transfers between devices: 183 us -> none  [body(): lax.psum_scatter(lax.dot_general(normed, pre_grad, (((0,), (0,)), ((), ()...]
    ppermute x3 -> x17, waiting for transfers between devices: 82.1 us -> 169 us  [the longest x6 90 us: line(): return lax.ppermute(value, axis, pairs)]
    psum x1 -> x0, waiting for transfers between devices: 83.4 us -> none  [body(): dnormed = lax.psum(dnormed_part, 'mp')]
    all_gather x3 -> x0, waiting for transfers between devices: 72.1 us -> none  [the longest x1 35.2 us: body(): lax.all_gather(act_saved[0], 'mp', axis=1, tiled=True)]
    ppermute x3 -> x17, starting transfers between devices: 1.52 us -> 32.2 us  [the longest x6 19.2 us: line(): return lax.ppermute(value, axis, pairs)]
    select_n x0 -> x5, other arithmetic: none -> 6.64 us  [the longest x2 3.81 us: whole_rows(): jnp.where(first, own, other)]
    reduce_sum x3, other arithmetic: 6.3 us -> 1.1 us  [normalize(): average = jnp.mean(values, axis=-1, keepdims=True)]
  transfers between devices with their start and end apart: 8 -> 17, of which waited for: 6 -> 11; matrix products, arithmetic and copies ran while one was open for 14% -> 11% of each run, Pallas kernels for 0% -> 0%
where the time goes in v1:
time: 281 us
  waiting for transfers between devices  169 us (60%)
  matrix products  52.8 us (19%)
  starting transfers between devices  32.2 us (11%)
  other arithmetic  15.7 us (6%)
  local copies, waits for them, and re-layouts  9.92 us (4%)
    ppermute x6, waiting for transfers between devices, line(): return lax.ppermute(value, axis, pairs)  90 us
    ppermute x10, waiting for transfers between devices, shift(): lax.ppermute(value, axis, [(at, (at + steps) % count) for at in range(cou...  64.9 us
    dot_general x2, matrix products, forward_layer(): preact = jnp.dot(normed, weight, preferred_element_type=jnp.float32)  22.7 us
    ppermute x6, starting transfers between devices, line(): return lax.ppermute(value, axis, pairs)  19.2 us
    ppermute x1, waiting for transfers between devices, shift_and_swap(): return lax.ppermute(value, ('section', 'mp'), pairs)  14.1 us
    dot_general x1, matrix products, body(): lax.dot_general(pre_grad, weight, (((1,), (1,)), ((), ())), preferred_ele...  13.9 us
    ppermute x10, starting transfers between devices, shift(): lax.ppermute(value, axis, [(at, (at + steps) % count) for at in range(cou...  10.2 us
    dot_general x1, matrix products, body(): preact = jnp.dot(normed, weight, preferred_element_type=jnp.float32)  9.49 us
  transfers between devices with their start and end apart: 17, of which 11 were waited for; matrix products, arithmetic and copies ran while one was open for 11% of the time, Pallas kernels for 0%

profile of v1, /device:TPU:8, one launch (start us, length us, event | category | flops | bytes accessed | tf_op | source)
XLA Modules:
  0.0 280.6 jit_solution(15631313648038799422)
XLA Ops:
  2.7 24.2 %collective-permute-done = bf16[256,2048]{1,0:T(8,128)(2,1)S(1)} collective-permute-done((bf16[256,2048]{1,0:T(8,128)(2,1)}, bf16[256,2048]{1,0:T(8,128)(2,1)S(1)}, u32[]{:S(2)}, u32[]{:S(2)}) %collective-permute-start) | collective-permute-done | bytes 1048608 | tf_op jit(solution)/shard_map/ppermute | solution.py:11
  29.5 10.9 %fusion.48 = bf16[256,2048]{1,0:T(8,128)(2,1)S(1)} fusion(bf16[1,4096,2048]{2,1,0:T(8,128)(2,1)} %param.5, f32[256]{0:T(256)S(1)} %add_rsqrt_fusion.2, f32[256]{0:T(256)S(1)} %broadcast_multiply_fusion.2, bf16[256,2048]{1,0:T(8,128)(2,1)S(1)} %get-tuple-element.16, bf16[256,2048]{1,0:T(8,128)(2,1)S(1)} %get-tuple-element.15, ...), kind=kOutput, calls=%fused_computation.57 | convolution fusion | flops 4308074496 | bytes 20973568 | tf_op jit(solution)/shard_map/dot_general | solution.py:50
  40.5 2.7 collective-permute-start.2
  43.2 5.1 %collective-permute-done.4 = bf16[256,2048]{1,0:T(8,128)(2,1)S(1)} collective-permute-done((bf16[256,2048]{1,0:T(8,128)(2,1)}, bf16[256,2048]{1,0:T(8,128)(2,1)S(1)}, u32[]{:S(2)}, u32[]{:S(2)}) %collective-permute-start.4) | collective-permute-done | bytes 1048608 | tf_op jit(solution)/shard_map/ppermute | solution.py:11
  48.3 6.4 %collective-permute-done.1 = bf16[256,2048]{1,0:T(8,128)(2,1)S(1)} collective-permute-done((bf16[256,2048]{1,0:T(8,128)(2,1)S(1)}, bf16[256,2048]{1,0:T(8,128)(2,1)S(1)}, u32[]{:S(2)}, u32[]{:S(2)}) %collective-permute-start.1) | collective-permute-done | bytes 1048608 | tf_op jit(solution)/shard_map/ppermute | solution.py:11
  55.7 14.1 %collective-permute-done.2 = bf16[256,2048]{1,0:T(8,128)(2,1)} collective-permute-done((bf16[256,2048]{1,0:T(8,128)(2,1)S(1)}, bf16[256,2048]{1,0:T(8,128)(2,1)}, u32[]{:S(2)}, u32[]{:S(2)}) %collective-permute-start.2) | collective-permute-done | bytes 1048608 | tf_op jit(solution)/shard_map/ppermute | solution.py:31
  75.5 9.5 %fusion.2 = f32[256,2048]{1,0:T(8,128)} fusion(bf16[256,4096]{1,0:T(8,128)(2,1)S(1)} %fusion.98, bf16[1,4096,2048]{2,1,0:T(8,128)(2,1)} %param.5), kind=kOutput, calls=%fused_computation.2 | convolution fusion | flops 4294967296 | bytes 20971520 | tf_op jit(solution)/shard_map/dot_general | solution.py:74
  85.0 13.9 %fusion.99 = (f32[256]{0:T(256)S(1)}, f32[256]{0:T(256)S(1)}, f32[256,4096]{1,0:T(8,128)}, f32[256,4096]{1,0:T(8,128)}) fusion(f32[256]{0:T(256)S(1)} %add_rsqrt_fusion, f32[256]{0:T(256)S(1)} %broadcast_multiply_fusion, bf16[256,2048]{1,0:T(8,128)(2,1)S(1)} %get-tuple-element.12, bf16[256,2048]{1,0:T(8,128)(2,1)S(1)} %get-tuple-element.11, ...), kind=kOutput, calls=%fused_computation.123 | convolution fusion | flops 4315414528 | bytes 30412800 | tf_op jit(solution)/shard_map/dot_general | solution.py:87
  98.9 2.8 dynamic-slice_convert_fusion
  103.8 24.2 %collective-permute-done.6 = f32[2,256]{1,0:T(2,128)S(1)} collective-permute-done((f32[2,256]{1,0:T(2,128)S(1)}, f32[2,256]{1,0:T(2,128)S(1)}, u32[]{:S(2)}, u32[]{:S(2)}) %collective-permute-start.6) | collective-permute-done | bytes 2080 | tf_op jit(solution)/shard_map/ppermute | solution.py:11
  128.1 5.0 %fusion.35 = (bf16[256,2048]{1,0:T(8,128)(2,1)S(1)}, bf16[256,2048]{1,0:T(8,128)(2,1)}) fusion(f32[256,2048]{1,0:T(8,128)} %fusion.2, bf16[1,256,2048]{2,1,0:T(8,128)(2,1)S(1)} %copy-done.4, f32[256]{0:T(256)S(1)} %bitcast.54, f32[256,4096]{1,0:T(8,128)} %get-tuple-element.6, s32[]{:T(128)S(6)} %select_n.87, f32[256]{0:T(256)S(1)} %bitcast.53, ...), kind=kLoop, calls=%fused_computation.48 | loop fusion | flops 15204352 | bytes 10488836 | tf_op jit(solution)/shard_map/convert_element_type | solution.py:76
  133.0 3.5 %collective-permute-start.11 = (bf16[256,2048]{1,0:T(8,128)(2,1)S(1)}, bf16[256,2048]{1,0:T(8,128)(2,1)S(1)}, u32[]{:S(2)}, u32[]{:S(2)}) collective-permute-start(bf16[256,2048]{1,0:T(8,128)(2,1)S(1)} %get-tuple-element.17), channel_id=1, source_target_pairs={{0,8},{8,16},{16,24},{1,9},{9,17},{17,25},{2,10},{10,18},{18,26},{... | collective-permute-start | bytes 3145736 | tf_op jit(solution)/shard_map/ppermute | solution.py:21
  140.0 20.0 %collective-permute-done.11 = bf16[256,2048]{1,0:T(8,128)(2,1)S(1)} collective-permute-done((bf16[256,2048]{1,0:T(8,128)(2,1)S(1)}, bf16[256,2048]{1,0:T(8,128)(2,1)S(1)}, u32[]{:S(2)}, u32[]{:S(2)}) %collective-permute-start.11) | collective-permute-done | bytes 1048608 | tf_op jit(solution)/shard_map/ppermute | solution.py:21
  160.0 3.7 %collective-permute-start.15 = (bf16[256,2048]{1,0:T(8,128)(2,1)S(1)}, bf16[256,2048]{1,0:T(8,128)(2,1)}, u32[]{:S(2)}, u32[]{:S(2)}) collective-permute-start(bf16[256,2048]{1,0:T(8,128)(2,1)S(1)} %collective-permute-done.11), channel_id=1, source_target_pairs={{0,8},{8,16},{16,24},{1,9},{9,17},{17,25},{2,10},{10,18},{18,26},{... | collective-permute-start | bytes 3145736 | tf_op jit(solution)/shard_map/ppermute | solution.py:21
  163.7 11.8 %add_convert_fusion = bf16[256,2048]{1,0:T(8,128)(2,1)} fusion(bf16[256,2048]{1,0:T(8,128)(2,1)S(1)} %copy-done.2, bf16[1,4096,2048]{2,1,0:T(8,128)(2,1)} %param.5, f32[256]{0:T(256)S(1)} %add_rsqrt_fusion.1, f32[256]{0:T(256)S(1)} %broadcast_multiply_fusion.1, bf16[256,2048]{1,0:T(8,128)(2,1)S(1)} %get-tuple-element.22, ...), kind=kOutput, calls=%fused_computation.80 | convolution fusion | flops 4308074496 | bytes 20973568 | tf_op jit(solution)/shard_map/dot_general | solution.py:50
  177.2 3.1 %collective-permute-start.13 = (bf16[256,2048]{1,0:T(8,128)(2,1)}, bf16[256,2048]{1,0:T(8,128)(2,1)}, u32[]{:S(2)}, u32[]{:S(2)}) collective-permute-start(bf16[256,2048]{1,0:T(8,128)(2,1)} %collective-permute-done.12), channel_id=1, source_target_pairs={{8,0},{16,8},{24,16},{9,1},{17,9},{25,17},{10,2},{18,10},{26,18},{... | collective-permute-start | bytes 3145736 | tf_op jit(solution)/shard_map/ppermute | solution.py:21
  180.3 6.1 %collective-permute-done.15 = bf16[256,2048]{1,0:T(8,128)(2,1)} collective-permute-done((bf16[256,2048]{1,0:T(8,128)(2,1)S(1)}, bf16[256,2048]{1,0:T(8,128)(2,1)}, u32[]{:S(2)}, u32[]{:S(2)}) %collective-permute-start.15) | collective-permute-done | bytes 1048608 | tf_op jit(solution)/shard_map/ppermute | solution.py:21
  186.4 3.5 %collective-permute-start.16 = (bf16[256,2048]{1,0:T(8,128)(2,1)}, bf16[256,2048]{1,0:T(8,128)(2,1)}, u32[]{:S(2)}, u32[]{:S(2)}) collective-permute-start(bf16[256,2048]{1,0:T(8,128)(2,1)} %collective-permute-done.15), channel_id=1, source_target_pairs={{0,8},{8,16},{16,24},{1,9},{9,17},{17,25},{2,10},{10,18},{18,26},{... | collective-permute-start | bytes 3145736 | tf_op jit(solution)/shard_map/ppermute | solution.py:21
  194.7 4.9 %collective-permute-done.7 = bf16[256,2048]{1,0:T(8,128)(2,1)S(1)} collective-permute-done((bf16[256,2048]{1,0:T(8,128)(2,1)}, bf16[256,2048]{1,0:T(8,128)(2,1)S(1)}, u32[]{:S(2)}, u32[]{:S(2)}) %collective-permute-start.7) | collective-permute-done | bytes 1048608 | tf_op jit(solution)/shard_map/ppermute | solution.py:11
  201.1 4.4 %collective-permute-done.13 = bf16[256,2048]{1,0:T(8,128)(2,1)} collective-permute-done((bf16[256,2048]{1,0:T(8,128)(2,1)}, bf16[256,2048]{1,0:T(8,128)(2,1)}, u32[]{:S(2)}, u32[]{:S(2)}) %collective-permute-start.13) | collective-permute-done | bytes 1048608 | tf_op jit(solution)/shard_map/ppermute | solution.py:21
  205.5 3.1 %collective-permute-start.14 = (bf16[256,2048]{1,0:T(8,128)(2,1)}, bf16[256,2048]{1,0:T(8,128)(2,1)S(1)}, u32[]{:S(2)}, u32[]{:S(2)}) collective-permute-start(bf16[256,2048]{1,0:T(8,128)(2,1)} %collective-permute-done.13), channel_id=1, source_target_pairs={{8,0},{16,8},{24,16},{9,1},{17,9},{25,17},{10,2},{18,10},{26,18},{... | collective-permute-start | bytes 3145736 | tf_op jit(solution)/shard_map/ppermute | solution.py:21
  210.0 25.8 %collective-permute-done.16 = bf16[256,2048]{1,0:T(8,128)(2,1)} collective-permute-done((bf16[256,2048]{1,0:T(8,128)(2,1)}, bf16[256,2048]{1,0:T(8,128)(2,1)}, u32[]{:S(2)}, u32[]{:S(2)}) %collective-permute-start.16) | collective-permute-done | bytes 1048608 | tf_op jit(solution)/shard_map/ppermute | solution.py:21
  237.2 33.7 %collective-permute-done.14 = bf16[256,2048]{1,0:T(8,128)(2,1)S(1)} collective-permute-done((bf16[256,2048]{1,0:T(8,128)(2,1)}, bf16[256,2048]{1,0:T(8,128)(2,1)S(1)}, u32[]{:S(2)}, u32[]{:S(2)}) %collective-permute-start.14) | collective-permute-done | bytes 1048608 | tf_op jit(solution)/shard_map/ppermute | solution.py:21
  271.0 6.7 %convert_bitcast_fusion = bf16[1,1024,2048]{2,1,0:T(8,128)(2,1)} fusion(bf16[256,2048]{1,0:T(8,128)(2,1)S(1)} %broadcast_select_fusion, bf16[256,2048]{1,0:T(8,128)(2,1)S(1)} %broadcast_select_fusion.1, bf16[256,2048]{1,0:T(8,128)(2,1)S(1)} %broadcast_select_fusion.2, bf16[256,2048]{1,0:T(8,128)(2,1)S(1)} %copy-done.6, ...), kind=kOutput, calls=%fused_computation.33 | convolution fusion | flops 4322230272 | bytes 10485760 | tf_op jit(solution)/shard_map/dot_general | solution.py:107
  (62 shorter events, 30.5 us)
Async XLA Ops:
  0.6 26.3 %collective-permute-start = (bf16[256,2048]{1,0:T(8,128)(2,1)}, bf16[256,2048]{1,0:T(8,128)(2,1)S(1)}, u32[]{:S(2)}, u32[]{:S(2)}) collective-permute-start(bf16[256,2048]{1,0:T(8,128)(2,1)} %bitcast.49), channel_id=1, source_target_pairs={{0,1},{1,0},{2,3},{3,2},{4,5},{5,4},{6,7},{7,6},{8,9},{9,8},{10,11... | collective-permute-start | bytes 3145736 | tf_op jit(solution)/shard_map/ppermute | solution.py:11
  2.2 46.1 %collective-permute-start.4 = (bf16[256,2048]{1,0:T(8,128)(2,1)}, bf16[256,2048]{1,0:T(8,128)(2,1)S(1)}, u32[]{:S(2)}, u32[]{:S(2)}) collective-permute-start(bf16[256,2048]{1,0:T(8,128)(2,1)} %bitcast.50), channel_id=1, source_target_pairs={{0,1},{1,0},{2,3},{3,2},{4,5},{5,4},{6,7},{7,6},{8,9},{9,8},{10,11... | collective-permute-start | bytes 3145736 | tf_op jit(solution)/shard_map/ppermute | solution.py:11
  40.4 14.3 %collective-permute-start.1 = (bf16[256,2048]{1,0:T(8,128)(2,1)S(1)}, bf16[256,2048]{1,0:T(8,128)(2,1)S(1)}, u32[]{:S(2)}, u32[]{:S(2)}) collective-permute-start(bf16[256,2048]{1,0:T(8,128)(2,1)S(1)} %fusion.48), channel_id=1, source_target_pairs={{0,2},{2,4},{4,6},{6,0},{1,3},{3,5},{5,7},{7,1},{8,10},{10,12},{12... | collective-permute-start | bytes 3145736 | tf_op jit(solution)/shard_map/ppermute | solution.py:11
  40.5 29.3 %collective-permute-start.2 = (bf16[256,2048]{1,0:T(8,128)(2,1)S(1)}, bf16[256,2048]{1,0:T(8,128)(2,1)}, u32[]{:S(2)}, u32[]{:S(2)}) collective-permute-start(bf16[256,2048]{1,0:T(8,128)(2,1)S(1)} %fusion.48), channel_id=1, source_target_pairs={{0,3},{1,2},{2,5},{3,4},{4,7},{5,6},{6,1},{7,0},{8,11},{9,10},{10,... | collective-permute-start | bytes 3145736 | tf_op jit(solution)/shard_map/ppermute | solution.py:31
  48.3 6.4 %copy-start.7 = (bf16[256,2048]{1,0:T(8,128)(2,1)}, bf16[256,2048]{1,0:T(8,128)(2,1)S(1)}, u32[]{:S(2)}) copy-start(bf16[256,2048]{1,0:T(8,128)(2,1)S(1)} %collective-permute-done.4) | copy-start | bytes 3145732
  98.9 29.1 %copy-start.4 = (bf16[1,256,2048]{2,1,0:T(8,128)(2,1)S(1)}, bf16[1,256,2048]{2,1,0:T(8,128)(2,1)}, u32[]{:S(2)}) copy-start(bf16[1,256,2048]{2,1,0:T(8,128)(2,1)} %param.7) | copy-start | bytes 3145732
  101.7 26.3 %collective-permute-start.5 = (bf16[256,2048]{1,0:T(8,128)(2,1)}, bf16[256,2048]{1,0:T(8,128)(2,1)}, u32[]{:S(2)}, u32[]{:S(2)}) collective-permute-start(bf16[256,2048]{1,0:T(8,128)(2,1)} %dynamic-slice_convert_fusion), channel_id=1, source_target_pairs={{0,1},{1,0},{2,3},{3,2},{4,5},{5,4},{6,7},{7,6},{8,9},{9,8},{10,11... | collective-permute-start | bytes 3145736 | tf_op jit(solution)/shard_map/ppermute | solution.py:11
  102.2 25.8 %collective-permute-start.6 = (f32[2,256]{1,0:T(2,128)S(1)}, f32[2,256]{1,0:T(2,128)S(1)}, u32[]{:S(2)}, u32[]{:S(2)}) collective-permute-start(f32[2,256]{1,0:T(2,128)S(1)} %pad_maximum_fusion.5), channel_id=1, source_target_pairs={{0,1},{1,0},{2,3},{3,2},{4,5},{5,4},{6,7},{7,6},{8,9},{9,8},{10,11... | collective-permute-start | bytes 6152 | tf_op jit(solution)/shard_map/ppermute | solution.py:11
  133.0 4.6 %copy-start.5 = (bf16[256,2048]{1,0:T(8,128)(2,1)}, bf16[256,2048]{1,0:T(8,128)(2,1)S(1)}, u32[]{:S(2)}) copy-start(bf16[256,2048]{1,0:T(8,128)(2,1)S(1)} %get-tuple-element.17) | copy-start | bytes 3145732
  133.0 27.0 %collective-permute-start.11 = (bf16[256,2048]{1,0:T(8,128)(2,1)S(1)}, bf16[256,2048]{1,0:T(8,128)(2,1)S(1)}, u32[]{:S(2)}, u32[]{:S(2)}) collective-permute-start(bf16[256,2048]{1,0:T(8,128)(2,1)S(1)} %get-tuple-element.17), channel_id=1, source_target_pairs={{0,8},{8,16},{16,24},{1,9},{9,17},{17,25},{2,10},{10,18},{18,26},{... | collective-permute-start | bytes 3145736 | tf_op jit(solution)/shard_map/ppermute | solution.py:21
  136.5 27.2 %copy-start.2 = (bf16[256,2048]{1,0:T(8,128)(2,1)S(1)}, bf16[256,2048]{1,0:T(8,128)(2,1)}, u32[]{:S(2)}) copy-start(bf16[256,2048]{1,0:T(8,128)(2,1)} %copy-done.1) | copy-start | bytes 3145732
  137.6 39.6 %collective-permute-start.12 = (bf16[256,2048]{1,0:T(8,128)(2,1)S(1)}, bf16[256,2048]{1,0:T(8,128)(2,1)}, u32[]{:S(2)}, u32[]{:S(2)}) collective-permute-start(bf16[256,2048]{1,0:T(8,128)(2,1)S(1)} %get-tuple-element.17), channel_id=1, source_target_pairs={{8,0},{16,8},{24,16},{9,1},{17,9},{25,17},{10,2},{18,10},{26,18},{... | collective-permute-start | bytes 3145736 | tf_op jit(solution)/shard_map/ppermute | solution.py:21
  160.0 15.6 %copy-start.8 = (bf16[256,2048]{1,0:T(8,128)(2,1)}, bf16[256,2048]{1,0:T(8,128)(2,1)S(1)}, u32[]{:S(2)}) copy-start(bf16[256,2048]{1,0:T(8,128)(2,1)S(1)} %collective-permute-done.11) | copy-start | bytes 3145732
  160.0 26.4 %collective-permute-start.15 = (bf16[256,2048]{1,0:T(8,128)(2,1)S(1)}, bf16[256,2048]{1,0:T(8,128)(2,1)}, u32[]{:S(2)}, u32[]{:S(2)}) collective-permute-start(bf16[256,2048]{1,0:T(8,128)(2,1)S(1)} %collective-permute-done.11), channel_id=1, source_target_pairs={{0,8},{8,16},{16,24},{1,9},{9,17},{17,25},{2,10},{10,18},{18,26},{... | collective-permute-start | bytes 3145736 | tf_op jit(solution)/shard_map/ppermute | solution.py:21
  175.6 17.5 %collective-permute-start.3 = (bf16[256,2048]{1,0:T(8,128)(2,1)}, bf16[256,2048]{1,0:T(8,128)(2,1)S(1)}, u32[]{:S(2)}, u32[]{:S(2)}) collective-permute-start(bf16[256,2048]{1,0:T(8,128)(2,1)} %add_convert_fusion), channel_id=1, source_target_pairs={{0,6},{2,0},{4,2},{6,4},{1,7},{3,1},{5,3},{7,5},{8,14},{10,8},{12,... | collective-permute-start | bytes 3145736 | tf_op jit(solution)/shard_map/ppermute | solution.py:11
  175.7 23.9 %collective-permute-start.7 = (bf16[256,2048]{1,0:T(8,128)(2,1)}, bf16[256,2048]{1,0:T(8,128)(2,1)S(1)}, u32[]{:S(2)}, u32[]{:S(2)}) collective-permute-start(bf16[256,2048]{1,0:T(8,128)(2,1)} %get-tuple-element.18), channel_id=1, source_target_pairs={{0,6},{2,0},{4,2},{6,4},{1,7},{3,1},{5,3},{7,5},{8,14},{10,8},{12,... | collective-permute-start | bytes 3145736 | tf_op jit(solution)/shard_map/ppermute | solution.py:11
  177.2 28.3 %collective-permute-start.13 = (bf16[256,2048]{1,0:T(8,128)(2,1)}, bf16[256,2048]{1,0:T(8,128)(2,1)}, u32[]{:S(2)}, u32[]{:S(2)}) collective-permute-start(bf16[256,2048]{1,0:T(8,128)(2,1)} %collective-permute-done.12), channel_id=1, source_target_pairs={{8,0},{16,8},{24,16},{9,1},{17,9},{25,17},{10,2},{18,10},{26,18},{... | collective-permute-start | bytes 3145736 | tf_op jit(solution)/shard_map/ppermute | solution.py:21
  186.4 49.4 %collective-permute-start.16 = (bf16[256,2048]{1,0:T(8,128)(2,1)}, bf16[256,2048]{1,0:T(8,128)(2,1)}, u32[]{:S(2)}, u32[]{:S(2)}) collective-permute-start(bf16[256,2048]{1,0:T(8,128)(2,1)} %collective-permute-done.15), channel_id=1, source_target_pairs={{0,8},{8,16},{16,24},{1,9},{9,17},{17,25},{2,10},{10,18},{18,26},{... | collective-permute-start | bytes 3145736 | tf_op jit(solution)/shard_map/ppermute | solution.py:21
  191.7 79.3 %collective-permute-start.10 = (bf16[256,1024]{1,0:T(8,128)(2,1)S(1)}, bf16[256,1024]{1,0:T(8,128)(2,1)S(1)}, u32[]{:S(2)}, u32[]{:S(2)}) collective-permute-start(bf16[256,1024]{1,0:T(8,128)(2,1)S(1)} %get-tuple-element.8), channel_id=1, source_target_pairs={{0,24},{8,0},{16,8},{24,16},{1,25},{9,1},{17,9},{25,17},{2,26},{10... | collective-permute-start | bytes 1572872 | tf_op jit(solution)/shard_map/ppermute | solution.py:11
  193.1 77.9 %collective-permute-start.9 = (bf16[256,1024]{1,0:T(8,128)(2,1)S(1)}, bf16[256,1024]{1,0:T(8,128)(2,1)S(1)}, u32[]{:S(2)}, u32[]{:S(2)}) collective-permute-start(bf16[256,1024]{1,0:T(8,128)(2,1)S(1)} %get-tuple-element.9), channel_id=1, source_target_pairs={{0,16},{8,24},{16,0},{24,8},{1,17},{9,25},{17,1},{25,9},{2,18},{10... | collective-permute-start | bytes 1572872 | tf_op jit(solution)/shard_map/ppermute | solution.py:11
  199.6 71.4 %collective-permute-start.8 = (bf16[256,1024]{1,0:T(8,128)(2,1)S(1)}, bf16[256,1024]{1,0:T(8,128)(2,1)S(1)}, u32[]{:S(2)}, u32[]{:S(2)}) collective-permute-start(bf16[256,1024]{1,0:T(8,128)(2,1)S(1)} %get-tuple-element.10), channel_id=1, source_target_pairs={{0,8},{8,16},{16,24},{24,0},{1,9},{9,17},{17,25},{25,1},{2,10},{10... | collective-permute-start | bytes 1572872 | tf_op jit(solution)/shard_map/ppermute | solution.py:11
  205.5 65.4 %collective-permute-start.14 = (bf16[256,2048]{1,0:T(8,128)(2,1)}, bf16[256,2048]{1,0:T(8,128)(2,1)S(1)}, u32[]{:S(2)}, u32[]{:S(2)}) collective-permute-start(bf16[256,2048]{1,0:T(8,128)(2,1)} %collective-permute-done.13), channel_id=1, source_target_pairs={{8,0},{16,8},{24,16},{9,1},{17,9},{25,17},{10,2},{18,10},{26,18},{... | collective-permute-start | bytes 3145736 | tf_op jit(solution)/shard_map/ppermute | solution.py:21
  210.0 60.9 %copy-start.9 = (bf16[256,2048]{1,0:T(8,128)(2,1)S(1)}, bf16[256,2048]{1,0:T(8,128)(2,1)}, u32[]{:S(2)}) copy-start(bf16[256,2048]{1,0:T(8,128)(2,1)} %copy-done.8) | copy-start | bytes 3145732
  237.2 33.9 %copy-start.6 = (bf16[256,2048]{1,0:T(8,128)(2,1)S(1)}, bf16[256,2048]{1,0:T(8,128)(2,1)}, u32[]{:S(2)}) copy-start(bf16[256,2048]{1,0:T(8,128)(2,1)} %copy-done.5) | copy-start | bytes 3145732
  (3 other events, 3.5 us)

commit v2 on v1

v2 whole, which is shorter than its diff:
```python
import functools

import jax
import jax.numpy as jnp
from jax import lax
from jax.experimental import pallas as pl
from jax.experimental.pallas import tpu as pltpu
from jax.sharding import PartitionSpec as P

EPS = 1e-05
BF16 = jnp.bfloat16
F32 = jnp.float32
VMEM_LIMIT = 12 * 2**20
CHUNKS = 2


def shift(value, axis, steps):
    count = lax.axis_size(axis)
    return lax.ppermute(value, axis, [(at, (at + steps) % count) for at in range(count)])


def swap(value, axis):
    return shift(value, axis, 1)


def line(value, axis, steps):
    count = lax.axis_size(axis)
    pairs = [(at, at + steps) for at in range(count) if 0 <= at + steps < count]
    return lax.ppermute(value, axis, pairs)


def shift_and_swap(value, steps):
    sections, halves = lax.axis_size("section"), lax.axis_size("mp")
    pairs = [
        (at * halves + half, ((at + steps) % sections) * halves + (half + 1) % halves)
        for at in range(sections)
        for half in range(halves)
    ]
    return lax.ppermute(value, ("section", "mp"), pairs)


VMEM = pl.BlockSpec(memory_space=pltpu.VMEM)
SMEM = pl.BlockSpec(memory_space=pltpu.SMEM)
ANY = pl.BlockSpec(memory_space=pl.ANY)


def call(kernel, name, place, values, outs, tokens=(), scratch=(), limit=VMEM_LIMIT):
    counted = len(values)

    def run(place_ref, *refs):
        kernel(place_ref, *refs[:counted], *refs[counted + len(tokens) :])

    return pl.pallas_call(
        run,
        in_specs=[SMEM] + [VMEM] * len(values) + [ANY] * len(tokens),
        out_specs=[VMEM] * len(outs),
        out_shape=outs,
        scratch_shapes=scratch,
        compiler_params=pltpu.CompilerParams(vmem_limit_bytes=limit),
        cost_estimate=pl.CostEstimate(flops=1000, bytes_accessed=1000, transcendentals=0),
        name=name,
    )(place, *values, *tokens)


def array(rows, columns, dtype=BF16):
    return jax.ShapeDtypeStruct((rows, columns), dtype)


def gelu(v):
    scale = 0.7978845608028654
    return 0.5 * v * (1.0 + jnp.tanh(scale * (v + 0.044715 * (v * v * v))))


def gelu_slope(v):
    scale = 0.7978845608028654
    square = v * v
    t = jnp.tanh(scale * (v + 0.044715 * (square * v)))
    return 0.5 * (1.0 + t) + 0.5 * v * (1.0 - t * t) * (scale * (1.0 + 3 * 0.044715 * square))


def normalize_into(own_ref, other_ref, normed_ref, half, own_start=0, step=128):
    rows, columns = other_ref.shape
    own_at = pl.multiple_of(half * columns, columns)
    other_at = pl.multiple_of((1 - half) * columns, columns)
    inverses = []
    for start in range(0, rows, step):
        at = slice(start, start + step)
        own = own_ref[own_start + start : own_start + start + step, :].astype(F32)
        other = other_ref[at, :].astype(F32)
        total = jnp.sum(own, axis=-1, keepdims=True) + jnp.sum(other, axis=-1, keepdims=True)
        average = total / (2 * columns)
        own, other = own - average, other - average
        total = jnp.sum(own * own, axis=-1, keepdims=True)
        total = total + jnp.sum(other * other, axis=-1, keepdims=True)
        inverse = lax.rsqrt(total / (2 * columns) + EPS)
        normed_ref[at, pl.ds(own_at, columns)] = (own * inverse).astype(BF16)
        normed_ref[at, pl.ds(other_at, columns)] = (other * inverse).astype(BF16)
        inverses.append(inverse)
    return inverses


def norm_kernel(replicas, chunk, place_ref, own_ref, other_ref, normed_ref, inverse_ref, *block_refs):
    rows = other_ref.shape[0]
    (inverse,) = normalize_into(own_ref, other_ref, normed_ref, place_ref[1], chunk * rows, rows)
    inverse_ref[...] = jnp.broadcast_to(inverse, inverse_ref.shape)
    block = block_refs[0].shape[1]
    for steps in range(replicas):
        target = lax.rem(place_ref[0] + steps, replicas)
        block_refs[steps][...] = normed_ref[:, pl.ds(pl.multiple_of(target * block, block), block)]


def norm_blocks(place, own, other, replicas, chunk, tokens=()):
    rows, columns = other.shape
    outs = [array(rows, 2 * columns), array(rows, 128, F32)]
    outs += [array(rows, 2 * columns // replicas)] * replicas
    kernel = functools.partial(norm_kernel, replicas, chunk)
    return call(kernel, "norm_blocks", place, [own, other], outs, tokens)


def later_kernel(place_ref, value_ref, *refs):
    refs[-1][...] = value_ref[...]


def later(place, value, tokens):
    return call(later_kernel, "later", place, [value], [array(*value.shape)], tokens)[0]


def load_kernel(place_ref, weight_ref, held_ref, sem):
    copy = pltpu.make_async_copy(weight_ref, held_ref, sem)
    copy.start()
    copy.wait()


def load(place, weight):
    held = pl.pallas_call(
        load_kernel,
        in_specs=[SMEM, ANY],
        out_specs=VMEM,
        out_shape=pltpu.VMEM(weight.shape, weight.dtype),
        scratch_shapes=[pltpu.SemaphoreType.DMA],
        compiler_params=pltpu.CompilerParams(vmem_limit_bytes=VMEM_LIMIT),
        name="load_weights",
    )(place, weight)
    return pltpu.with_memory_space_constraint(held, pltpu.VMEM)


def pre_grad_kernel(chunk, place_ref, normed_ref, weight_ref, cot_ref, grad_ref, tile=256):
    rows = grad_ref.shape[0]
    for start in range(0, grad_ref.shape[1], tile):
        at = slice(start, start + tile)
        preact = jnp.dot(normed_ref[...], weight_ref[:, at], preferred_element_type=F32)
        cot = cot_ref[chunk * rows : (chunk + 1) * rows, at].astype(F32)
        grad_ref[:, at] = (cot * gelu_slope(preact)).astype(BF16)


def pre_grads(place, normed, weight, cot, chunk, tokens=()):
    outs = [array(normed.shape[0], weight.shape[1])]
    kernel = functools.partial(pre_grad_kernel, chunk)
    return call(kernel, "pre_grads", place, [normed, weight, cot], outs, tokens)[0]


def forward_kernel(place_ref, own_ref, other_ref, weight_ref, out_ref, normed_ref, tile=256):
    normalize_into(own_ref, other_ref, normed_ref, place_ref[1])
    for start in range(0, out_ref.shape[1], tile):
        at = slice(start, start + tile)
        preact = jnp.dot(normed_ref[...], weight_ref[:, at], preferred_element_type=F32)
        out_ref[:, at] = (own_ref[:, at].astype(F32) + gelu(preact)).astype(BF16)


def forward_layer(place, own, other, weight, tokens=()):
    scratch = [pltpu.VMEM((own.shape[0], weight.shape[0]), BF16)]
    return call(
        forward_kernel, "forward_layer", place, [own, other, weight], [array(*own.shape)], tokens, scratch
    )[0]


def dnormed_kernel(chunks, place_ref, *refs, tile=512):
    grad_refs, normed_refs = refs[:chunks], refs[chunks : 2 * chunks]
    weight_ref, send_ref, keep_ref, sums_ref = refs[2 * chunks :]
    rows = grad_refs[0].shape[0]
    depth, columns = weight_ref.shape
    lane = lax.broadcasted_iota(jnp.int32, (rows, sums_ref.shape[1]), 1)
    for chunk in range(chunks):
        at = slice(chunk * rows, (chunk + 1) * rows)
        first = second = jnp.zeros((rows, 1), F32)
        for mine in (False, True):
            half = place_ref[1] if mine else 1 - place_ref[1]
            for start in range(0, columns, tile):
                features = pl.ds(pl.multiple_of(half * columns + start, tile), tile)
                part = lax.dot_general(
                    grad_refs[chunk][...],
                    weight_ref[features, :],
                    (((1,), (1,)), ((), ())),
                    preferred_element_type=F32,
                )
                first += jnp.sum(part, axis=-1, keepdims=True)
                scaled = normed_refs[chunk][:, features].astype(F32)
                second += jnp.sum(part * scaled, axis=-1, keepdims=True)
                if mine:
                    keep_ref[at, start : start + tile] = part
                else:
                    send_ref[at, start : start + tile] = part.astype(BF16)
        sums_ref[at, :] = jnp.where(lane < 64, first, second)


def dnormed_parts(place, grads, normeds, weight, tokens=()):
    chunks = len(grads)
    rows, columns = chunks * grads[0].shape[0], weight.shape[1]
    outs = [array(rows, columns), array(rows, columns, F32), array(rows, 128, F32)]
    kernel = functools.partial(dnormed_kernel, chunks)
    return call(kernel, "dnormed_parts", place, [*grads, *normeds, weight], outs, tokens)


def input_grad_kernel(chunks, place_ref, cot_ref, keep_ref, arrived_ref, sums_ref, other_sums_ref, *refs):
    inverse_refs, normed_refs, out_ref = refs[:chunks], refs[chunks : 2 * chunks], refs[-1]
    rows = inverse_refs[0].shape[0]
    columns = cot_ref.shape[1]
    depth = 2 * columns
    mine = pl.ds(pl.multiple_of(place_ref[1] * columns, columns), columns)
    for chunk in range(chunks):
        at = slice(chunk * rows, (chunk + 1) * rows)
        sums = (sums_ref[at, :] + other_sums_ref[at, :]) / depth
        first, second = sums[:, 0:1], sums[:, 64:65]
        dnormed = keep_ref[at, :] + arrived_ref[at, :].astype(F32)
        scaled = normed_refs[chunk][:, mine].astype(F32)
        out_ref[at, :] = (
            cot_ref[at, :].astype(F32)
            + inverse_refs[chunk][:, 0:1] * (dnormed - first - scaled * second)
        ).astype(BF16)


def input_grads(place, cot, keep, arrived, sums, other_sums, inverses, normeds, tokens=()):
    values = [cot, keep, arrived, sums, other_sums, *inverses, *normeds]
    kernel = functools.partial(input_grad_kernel, len(inverses))
    return call(kernel, "input_grads", place, values, [array(*cot.shape)], tokens)[0]


def weight_grad_kernel(replicas, chunks, place_ref, *refs, tile=256):
    count = replicas * chunks
    block_refs, up_refs, down_refs = refs[:count], refs[count : 2 * count], refs[2 * count : -3]
    out_ref, blocks, grads = refs[-3:]
    rows = block_refs[0].shape[0]
    for index in range(count):
        at = slice(index * rows, (index + 1) * rows)
        blocks[at, :] = block_refs[index][...]
        steps = index // chunks
        if steps == 0:
            grads[at, :] = up_refs[index][...]
        else:
            grads[at, :] = jnp.where(
                place_ref[0] >= steps, up_refs[index][...], down_refs[index - chunks][...]
            )
    for start in range(0, out_ref.shape[0], tile):
        at = slice(start, start + tile)
        out_ref[at, :] = lax.dot_general(
            blocks[:, at], grads[...], (((0,), (0,)), ((), ())), preferred_element_type=F32
        ).astype(BF16)


def weight_grads(place, blocks, ups, downs, replicas, chunks, tokens=()):
    rows, depth = blocks[0].shape
    columns = ups[0].shape[1]
    count = replicas * chunks
    scratch = [pltpu.VMEM((count * rows, depth), BF16), pltpu.VMEM((count * rows, columns), BF16)]
    kernel = functools.partial(weight_grad_kernel, replicas, chunks)
    values = [*blocks, *ups, *downs[chunks:]]
    return call(kernel, "weight_grads", place, values, [array(depth, columns)], tokens, scratch, 28 * 2**20)[0]


def body(act_in, weights, act_saved, cotangent):
    weight = weights[0]
    own_in, own_saved, own_cot = act_in[0], act_saved[0], cotangent[0]
    rows = own_saved.shape[0] // CHUNKS
    replicas = lax.axis_size("dp")
    place = jnp.stack([lax.axis_index("dp"), lax.axis_index("mp")]).astype(jnp.int32)

    other_saved = [swap(own_saved[chunk * rows : (chunk + 1) * rows], "mp") for chunk in range(CHUNKS)]
    weight = load(place, weight)

    normeds, inverses, blocks, ups, downs = [], [], [], [], []
    tokens = [weight]
    for chunk in range(CHUNKS):
        normed, inverse, own_block, *away = norm_blocks(
            place, own_saved, other_saved[chunk], replicas, chunk, tokens
        )
        normeds.append(normed)
        inverses.append(inverse)
        blocks.append([own_block] + [shift(value, "dp", steps + 1) for steps, value in enumerate(away)])
        if chunk == 0:
            other_in = swap(later(place, own_in, [inverse]), "mp")
        pre_grad = pre_grads(place, normed, weight, own_cot, chunk)
        up, down = [pre_grad], [pre_grad]
        for _ in range(1, replicas):
            up.append(line(up[-1], "dp", 1))
            down.append(line(down[-1], "dp", -1))
        ups.append(up)
        downs.append(down)
        tokens = blocks[0][1:2]

    send, keep, sums = dnormed_parts(place, [up[0] for up in ups], normeds, weight, blocks[0][2:])
    arrived, other_sums = swap(send, "mp"), swap(sums, "mp")

    forward = forward_layer(place, own_in, other_in, weight, [ups[0][1], downs[0][1]])
    received = shift(forward, "section", 1)
    received_other = shift_and_swap(forward, 1)

    input_grad = input_grads(
        place, own_cot, keep, arrived, sums, other_sums, inverses, normeds, blocks[1][1:]
    )
    grad_back = shift(input_grad, "section", -1)

    shadow_there = forward_layer(
        place,
        received,
        received_other,
        weight,
        [ups[1][1], downs[1][1], ups[0][2], downs[0][2], input_grad],
    )
    shadow = shift(shadow_there, "section", -1)

    order = [(steps, chunk) for steps in range(replicas) for chunk in range(CHUNKS)]
    weight_grad = weight_grads(
        place,
        [blocks[chunk][steps] for steps, chunk in order],
        [ups[chunk][steps] for steps, chunk in order],
        [downs[chunk][(replicas - steps) % replicas] for steps, chunk in order],
        replicas,
        CHUNKS,
        [shadow_there],
    )
    return (received[None], shadow[None], grad_back[None], weight_grad[None])


def solution(mesh):
    return jax.shard_map(
        body,
        mesh=mesh,
        in_specs=(
            P("section", "dp", "mp"),
            P("section", None, "mp"),
            P("section", "dp", "mp"),
            P("section", "dp", "mp"),
        ),
        out_specs=(
            P("section", "dp", "mp"),
            P("section", "dp", "mp"),
            P("section", "dp", "mp"),
            P("section", "dp", "mp"),
        ),
        check_vma=False,
    )
```

time: 281 us -> 162 us (0.58)
  waiting for transfers between devices: 169 us -> 47.2 us
  matrix products: 52.8 us -> 0 us
  Pallas kernels: 0 us -> 46.4 us
  starting transfers between devices: 32.2 us -> 55.3 us
  other arithmetic: 15.7 us -> 0.07 us
    ppermute x6 -> x12, waiting for transfers between devices: 90 us -> 27.4 us  [line(): return lax.ppermute(value, axis, pairs)]
    dot_general x5 -> x0, matrix products: 52.8 us -> none  [the longest x2 22.7 us: forward_layer(): preact = jnp.dot(normed, weight, preferred_element_type=jnp.float32)]
    pallas_call x0 -> x11, Pallas kernels: none -> 46.4 us  [the longest x10 44.7 us: call(): pl.pallas_call(run, in_specs=[SMEM] + [VMEM] * len(values) + [ANY] * len(...]
    ppermute x10 -> x14, waiting for transfers between devices: 64.9 us -> 19.8 us  [shift(): lax.ppermute(value, axis, [(at, (at + steps) % count) for at in range(cou...]
    ppermute x6 -> x12, starting transfers between devices: 19.2 us -> 34.9 us  [line(): return lax.ppermute(value, axis, pairs)]
    ppermute x1, waiting for transfers between devices: 14.1 us -> 0.01 us  [shift_and_swap(): return lax.ppermute(value, ('section', 'mp'), pairs)]
    ppermute x10 -> x14, starting transfers between devices: 10.2 us -> 17.7 us  [shift(): lax.ppermute(value, axis, [(at, (at + steps) % count) for at in range(cou...]
    select_n x5 -> x0, other arithmetic: 6.64 us -> none  [the longest x2 3.81 us: whole_rows(): jnp.where(first, own, other)]
  transfers between devices with their start and end apart: 17 -> 27, of which waited for: 11 -> 8; matrix products, arithmetic and copies ran while one was open for 11% -> 0% of each run, Pallas kernels for 0% -> 29%
where the time goes in v2:
time: 162 us; the launch traced here: 160 us
  starting transfers between devices  55.3 us (34%)
  waiting for transfers between devices  47.2 us (29%)
  Pallas kernels  46.4 us (29%)
  local copies, waits for them, and re-layouts  9.97 us (6%)
    pallas_call x10, Pallas kernels, call(): pl.pallas_call(run, in_specs=[SMEM] + [VMEM] * len(values) + [ANY] * len(...  44.7 us
    ppermute x12, starting transfers between devices, line(): return lax.ppermute(value, axis, pairs)  34.9 us
    ppermute x12, waiting for transfers between devices, line(): return lax.ppermute(value, axis, pairs)  27.4 us
    ppermute x14, waiting for transfers between devices, shift(): lax.ppermute(value, axis, [(at, (at + steps) % count) for at in range(cou...  19.8 us
    ppermute x14, starting transfers between devices, shift(): lax.ppermute(value, axis, [(at, (at + steps) % count) for at in range(cou...  17.7 us
    unnamed x11, local copies, waits for them, and re-layouts  8.7 us
  transfers between devices with their start and end apart: 27, of which 8 were waited for; matrix products, arithmetic and copies ran while one was open for 0% of the time, Pallas kernels for 29%

profile of v2, /device:TPU:8, one launch (start us, length us, event | category | flops | bytes accessed | tf_op | source)
XLA Modules:
  0.0 159.9 jit_solution(14028695482033967852)
XLA Ops:
  4.1 5.8 %copy-done = bf16[1,4096,2048]{2,1,0:T(8,128)(2,1)S(1)} copy-done((bf16[1,4096,2048]{2,1,0:T(8,128)(2,1)S(1)}, bf16[1,4096,2048]{2,1,0:T(8,128)(2,1)}, u32[]{:S(2)}) %copy-start) | copy-done | bytes 16777240
  11.6 5.2 %collective-permute-done.refs_1_ = bf16[128,2048]{1,0:T(8,128)(2,1)S(1)} collective-permute-done((bf16[128,2048]{1,0:T(8,128)(2,1)S(1)}, bf16[128,2048]{1,0:T(8,128)(2,1)S(1)}, u32[]{:S(2)}, u32[]{:S(2)}) %collective-permute-start) | collective-permute-done | bytes 524320 | tf_op jit(solution)/shard_map/ppermute | solution.py:19
  24.9 3.5 %pre_grads.2.refs_0_.refs_8_ = bf16[128,2048]{1,0:T(8,128)(2,1)S(1)} custom-call(s32[2]{0:T(128)S(1)} %pad_add_fusion.place_ref, bf16[128,4096]{1,0:T(8,128)(2,1)S(1)} %get-tuple-element.20.refs_0_.refs_2_.refs_7_, bf16[4096,2048]{1,0:T(8,128)(2,1)S(1)} %load_weights.1.refs_2_.refs_1_.refs_4_, bf16[256,2048]{1,0:T(8,128)(2,1)S(1)} %bitcast.15), custom_call_target="tpu_custom_call" | custom-call | flops 1000 | bytes 1000 | tf_op jit(solution)/shard_map/pre_grads/pallas_call | solution.py:53
  28.4 3.1 %collective-permute-start.2 = (bf16[128,2048]{1,0:T(8,128)(2,1)S(1)}, bf16[128,2048]{1,0:T(8,128)(2,1)S(1)}, u32[]{:S(2)}, u32[]{:S(2)}) collective-permute-start(bf16[128,2048]{1,0:T(8,128)(2,1)S(1)} %pre_grads.2.refs_0_.refs_8_), channel_id=1, source_target_pairs={{0,8},{8,16},{16,24},{1,9},{9,17},{17,25},{2,10},{10,18},{18,26},{... | collective-permute-start | bytes 1572872 | tf_op jit(solution)/shard_map/ppermute | solution.py:29
  31.5 6.9 %collective-permute-done.7.refs_2_ = bf16[128,1024]{1,0:T(8,128)(2,1)S(1)} collective-permute-done((bf16[128,1024]{1,0:T(8,128)(2,1)S(1)}, bf16[128,1024]{1,0:T(8,128)(2,1)S(1)}, u32[]{:S(2)}, u32[]{:S(2)}) %collective-permute-start.7) | collective-permute-done | bytes 262176 | tf_op jit(solution)/shard_map/ppermute | solution.py:19
  41.6 3.2 %collective-permute-done.12.refs_5_.refs_4_ = bf16[128,1024]{1,0:T(8,128)(2,1)S(1)} collective-permute-done((bf16[128,1024]{1,0:T(8,128)(2,1)S(1)}, bf16[128,1024]{1,0:T(8,128)(2,1)S(1)}, u32[]{:S(2)}, u32[]{:S(2)}) %collective-permute-start.12) | collective-permute-done | bytes 262176 | tf_op jit(solution)/shard_map/ppermute | solution.py:19
  44.8 3.5 %pre_grads.3.refs_1_.refs_9_ = bf16[128,2048]{1,0:T(8,128)(2,1)S(1)} custom-call(s32[2]{0:T(128)S(1)} %pad_add_fusion.place_ref, bf16[128,4096]{1,0:T(8,128)(2,1)S(1)} %get-tuple-element.22.refs_0_.refs_3_.refs_8_, bf16[4096,2048]{1,0:T(8,128)(2,1)S(1)} %load_weights.1.refs_2_.refs_1_.refs_4_, bf16[256,2048]{1,0:T(8,128)(2,1)S(1)} %bitcast.16), custom_call_target="tpu_custom_call" | custom-call | flops 1000 | bytes 1000 | tf_op jit(solution)/shard_map/pre_grads/pallas_call | solution.py:53
  48.4 11.7 %dnormed_parts.1 = (bf16[256,2048]{1,0:T(8,128)(2,1)S(1)}, f32[256,2048]{1,0:T(8,128)S(1)}, f32[256,128]{1,0:T(8,128)S(1)}) custom-call(s32[2]{0:T(128)S(1)} %pad_add_fusion.place_ref, bf16[128,2048]{1,0:T(8,128)(2,1)S(1)} %pre_grads.2.refs_0_.refs_8_, bf16[128,2048]{1,0:T(8,128)(2,1)S(1)} %pre_grads.3.refs_1_.refs_9_, ...), custom_call_target="tpu_custom_call" | custom-call | flops 1000 | bytes 1000 | tf_op jit(solution)/shard_map/dnormed_parts/pallas_call | solution.py:53
  60.6 4.5 %collective-permute-done.15.refs_4_ = f32[256,128]{1,0:T(8,128)S(1)} collective-permute-done((f32[256,128]{1,0:T(8,128)S(1)}, f32[256,128]{1,0:T(8,128)S(1)}, u32[]{:S(2)}, u32[]{:S(2)}) %collective-permute-start.15) | collective-permute-done | bytes 131104 | tf_op jit(solution)/shard_map/ppermute | solution.py:19
  65.1 3.4 %collective-permute-start.17 = (bf16[128,1024]{1,0:T(8,128)(2,1)S(1)}, bf16[128,1024]{1,0:T(8,128)(2,1)S(1)}, u32[]{:S(2)}, u32[]{:S(2)}) collective-permute-start(bf16[128,1024]{1,0:T(8,128)(2,1)S(1)} %get-tuple-element.30), channel_id=1, source_target_pairs={{0,16},{8,24},{16,0},{24,8},{1,17},{9,25},{17,1},{25,9},{2,18},{10... | collective-permute-start | bytes 786440 | tf_op jit(solution)/shard_map/ppermute | solution.py:19
  72.4 4.2 %collective-permute-start.9 = (bf16[128,2048]{1,0:T(8,128)(2,1)S(1)}, bf16[128,2048]{1,0:T(8,128)(2,1)S(1)}, u32[]{:S(2)}, u32[]{:S(2)}) collective-permute-start(bf16[128,2048]{1,0:T(8,128)(2,1)S(1)} %pre_grads.3.refs_1_.refs_9_), channel_id=1, source_target_pairs={{8,0},{16,8},{24,16},{9,1},{17,9},{25,17},{10,2},{18,10},{26,18},{... | collective-permute-start | bytes 1572872 | tf_op jit(solution)/shard_map/ppermute | solution.py:29
  77.2 7.2 %forward_layer.2 = bf16[256,2048]{1,0:T(8,128)(2,1)S(1)} custom-call(s32[2]{0:T(128)S(1)} %pad_add_fusion.place_ref, bf16[256,2048]{1,0:T(8,128)(2,1)S(1)} %bitcast.21, bf16[256,2048]{1,0:T(8,128)(2,1)S(1)} %collective-permute-done.1.refs_1_, bf16[4096,2048]{1,0:T(8,128)(2,1)S(1)} %load_weights.1.refs_2_.refs_1_.refs_4_, ...), custom_call_target="tpu_custom_call" | custom-call | flops 1000 | bytes 1000 | tf_op jit(solution)/shard_map/forward_layer/pallas_call | solution.py:53
  84.5 2.7 %collective-permute-start.5 = (bf16[256,2048]{1,0:T(8,128)(2,1)S(1)}, bf16[256,2048]{1,0:T(8,128)(2,1)S(1)}, u32[]{:S(2)}, u32[]{:S(2)}) collective-permute-start(bf16[256,2048]{1,0:T(8,128)(2,1)S(1)} %forward_layer.2), channel_id=1, source_target_pairs={{0,3},{1,2},{2,5},{3,4},{4,7},{5,6},{6,1},{7,0},{8,11},{9,10},{10,... | collective-permute-start | bytes 3145736 | tf_op jit(solution)/shard_map/ppermute | solution.py:39
  87.2 2.1 %collective-permute-done.8.refs_3_.refs_11_ = bf16[128,2048]{1,0:T(8,128)(2,1)S(1)} collective-permute-done((bf16[128,2048]{1,0:T(8,128)(2,1)S(1)}, bf16[128,2048]{1,0:T(8,128)(2,1)S(1)}, u32[]{:S(2)}, u32[]{:S(2)}) %collective-permute-start.8) | collective-permute-done | bytes 524320 | tf_op jit(solution)/shard_map/ppermute | solution.py:29
  89.3 4.4 %collective-permute-start.10 = (bf16[128,2048]{1,0:T(8,128)(2,1)S(1)}, bf16[128,2048]{1,0:T(8,128)(2,1)S(1)}, u32[]{:S(2)}, u32[]{:S(2)}) collective-permute-start(bf16[128,2048]{1,0:T(8,128)(2,1)S(1)} %collective-permute-done.2.refs_3_.refs_10_), channel_id=1, source_target_pairs={{0,8},{8,16},{16,24},{1,9},{9,17},{17,25},{2,10},{10,18},{18,26},{... | collective-permute-start | bytes 1572872 | tf_op jit(solution)/shard_map/ppermute | solution.py:29
  95.6 7.2 %collective-permute-done.10.refs_5_.refs_12_ = bf16[128,2048]{1,0:T(8,128)(2,1)S(1)} collective-permute-done((bf16[128,2048]{1,0:T(8,128)(2,1)S(1)}, bf16[128,2048]{1,0:T(8,128)(2,1)S(1)}, u32[]{:S(2)}, u32[]{:S(2)}) %collective-permute-start.10) | collective-permute-done | bytes 524320 | tf_op jit(solution)/shard_map/ppermute | solution.py:29
  102.8 3.9 %collective-permute-start.21 = (bf16[128,2048]{1,0:T(8,128)(2,1)S(1)}, bf16[128,2048]{1,0:T(8,128)(2,1)S(1)}, u32[]{:S(2)}, u32[]{:S(2)}) collective-permute-start(bf16[128,2048]{1,0:T(8,128)(2,1)S(1)} %collective-permute-done.8.refs_3_.refs_11_), channel_id=1, source_target_pairs={{0,8},{8,16},{16,24},{1,9},{9,17},{17,25},{2,10},{10,18},{18,26},{... | collective-permute-start | bytes 1572872 | tf_op jit(solution)/shard_map/ppermute | solution.py:29
  108.7 3.9 %collective-permute-start.22 = (bf16[128,2048]{1,0:T(8,128)(2,1)S(1)}, bf16[128,2048]{1,0:T(8,128)(2,1)S(1)}, u32[]{:S(2)}, u32[]{:S(2)}) collective-permute-start(bf16[128,2048]{1,0:T(8,128)(2,1)S(1)} %collective-permute-done.10.refs_5_.refs_12_), channel_id=1, source_target_pairs={{0,8},{8,16},{16,24},{1,9},{9,17},{17,25},{2,10},{10,18},{18,26},{... | collective-permute-start | bytes 1572872 | tf_op jit(solution)/shard_map/ppermute | solution.py:29
  114.3 7.2 %forward_layer.3.refs_22_ = bf16[256,2048]{1,0:T(8,128)(2,1)S(1)} custom-call(s32[2]{0:T(128)S(1)} %pad_add_fusion.place_ref, bf16[256,2048]{1,0:T(8,128)(2,1)S(1)} %collective-permute-done.4.refs_0_, bf16[256,2048]{1,0:T(8,128)(2,1)S(1)} %collective-permute-done.5.refs_1_, bf16[4096,2048]{1,0:T(8,128)(2,1)S(1)} %load_weights.1.refs_2_.refs_1_.refs_4_, ...), custom_call_target="tpu_custom_call" | custom-call | flops 1000 | bytes 1000 | tf_op jit(solution)/shard_map/forward_layer/pallas_call | solution.py:53
  121.5 2.5 %collective-permute-start.19 = (bf16[256,2048]{1,0:T(8,128)(2,1)S(1)}, bf16[256,2048]{1,0:T(8,128)(2,1)S(1)}, u32[]{:S(2)}, u32[]{:S(2)}) collective-permute-start(bf16[256,2048]{1,0:T(8,128)(2,1)S(1)} %forward_layer.3.refs_22_), channel_id=1, source_target_pairs={{0,6},{2,0},{4,2},{6,4},{1,7},{3,1},{5,3},{7,5},{8,14},{10,8},{12,... | collective-permute-start | bytes 3145736 | tf_op jit(solution)/shard_map/ppermute | solution.py:19
  125.9 3.9 %collective-permute-start.23 = (bf16[128,2048]{1,0:T(8,128)(2,1)S(1)}, bf16[128,2048]{1,0:T(8,128)(2,1)S(1)}, u32[]{:S(2)}, u32[]{:S(2)}) collective-permute-start(bf16[128,2048]{1,0:T(8,128)(2,1)S(1)} %collective-permute-done.21.refs_13_), channel_id=1, source_target_pairs={{0,8},{8,16},{16,24},{1,9},{9,17},{17,25},{2,10},{10,18},{18,26},{... | collective-permute-start | bytes 1572872 | tf_op jit(solution)/shard_map/ppermute | solution.py:29
  131.8 8.9 %collective-permute-done.24.refs_16_ = bf16[128,2048]{1,0:T(8,128)(2,1)S(1)} collective-permute-done((bf16[128,2048]{1,0:T(8,128)(2,1)S(1)}, bf16[128,2048]{1,0:T(8,128)(2,1)S(1)}, u32[]{:S(2)}, u32[]{:S(2)}) %collective-permute-start.24) | collective-permute-done | bytes 524320 | tf_op jit(solution)/shard_map/ppermute | solution.py:29
  140.7 9.1 %collective-permute-done.26.refs_17_ = bf16[128,2048]{1,0:T(8,128)(2,1)S(1)} collective-permute-done((bf16[128,2048]{1,0:T(8,128)(2,1)S(1)}, bf16[128,2048]{1,0:T(8,128)(2,1)S(1)}, u32[]{:S(2)}, u32[]{:S(2)}) %collective-permute-start.26) | collective-permute-done | bytes 524320 | tf_op jit(solution)/shard_map/ppermute | solution.py:29
  149.9 7.1 %weight_grads.1 = bf16[1024,2048]{1,0:T(8,128)(2,1)} custom-call(s32[2]{0:T(128)S(1)} %pad_add_fusion.place_ref, bf16[128,1024]{1,0:T(8,128)(2,1)S(1)} %get-tuple-element.32.refs_0_, bf16[128,1024]{1,0:T(8,128)(2,1)S(1)} %get-tuple-element.33.refs_1_, bf16[128,1024]{1,0:T(8,128)(2,1)S(1)} %collective-permute-done.7.refs_2_, ...), custom_call_target="tpu_custom_call" | custom-call | flops 1000 | bytes 1000 | tf_op jit(solution)/shard_map/weight_grads/pallas_call | solution.py:53
  (54 shorter events, 33.8 us)
Async XLA Ops:
  1.9 14.9 %collective-permute-start = (bf16[128,2048]{1,0:T(8,128)(2,1)S(1)}, bf16[128,2048]{1,0:T(8,128)(2,1)S(1)}, u32[]{:S(2)}, u32[]{:S(2)}) collective-permute-start(bf16[128,2048]{1,0:T(8,128)(2,1)S(1)} %get-tuple-element.35), channel_id=1, source_target_pairs={{0,1},{1,0},{2,3},{3,2},{4,5},{5,4},{6,7},{7,6},{8,9},{9,8},{10,11... | collective-permute-start | bytes 1572872 | tf_op jit(solution)/shard_map/ppermute | solution.py:19
  3.5 24.9 %collective-permute-start.6 = (bf16[128,2048]{1,0:T(8,128)(2,1)S(1)}, bf16[128,2048]{1,0:T(8,128)(2,1)S(1)}, u32[]{:S(2)}, u32[]{:S(2)}) collective-permute-start(bf16[128,2048]{1,0:T(8,128)(2,1)S(1)} %get-tuple-element.34), channel_id=1, source_target_pairs={{0,1},{1,0},{2,3},{3,2},{4,5},{5,4},{6,7},{7,6},{8,9},{9,8},{10,11... | collective-permute-start | bytes 1572872 | tf_op jit(solution)/shard_map/ppermute | solution.py:19
  18.7 57.9 %collective-permute-start.1 = (bf16[256,2048]{1,0:T(8,128)(2,1)S(1)}, bf16[256,2048]{1,0:T(8,128)(2,1)S(1)}, u32[]{:S(2)}, u32[]{:S(2)}) collective-permute-start(bf16[256,2048]{1,0:T(8,128)(2,1)S(1)} %later.1), channel_id=1, source_target_pairs={{0,1},{1,0},{2,3},{3,2},{4,5},{5,4},{6,7},{7,6},{8,9},{9,8},{10,11... | collective-permute-start | bytes 3145736 | tf_op jit(solution)/shard_map/ppermute | solution.py:19
  20.3 18.2 %collective-permute-start.7 = (bf16[128,1024]{1,0:T(8,128)(2,1)S(1)}, bf16[128,1024]{1,0:T(8,128)(2,1)S(1)}, u32[]{:S(2)}, u32[]{:S(2)}) collective-permute-start(bf16[128,1024]{1,0:T(8,128)(2,1)S(1)} %get-tuple-element.21), channel_id=1, source_target_pairs={{0,8},{8,16},{16,24},{24,0},{1,9},{9,17},{17,25},{25,1},{2,10},{10... | collective-permute-start | bytes 786440 | tf_op jit(solution)/shard_map/ppermute | solution.py:19
  21.9 23.0 %collective-permute-start.12 = (bf16[128,1024]{1,0:T(8,128)(2,1)S(1)}, bf16[128,1024]{1,0:T(8,128)(2,1)S(1)}, u32[]{:S(2)}, u32[]{:S(2)}) collective-permute-start(bf16[128,1024]{1,0:T(8,128)(2,1)S(1)} %get-tuple-element.23), channel_id=1, source_target_pairs={{0,16},{8,24},{16,0},{24,8},{1,17},{9,25},{17,1},{25,9},{2,18},{10... | collective-permute-start | bytes 786440 | tf_op jit(solution)/shard_map/ppermute | solution.py:19
  23.1 25.3 %collective-permute-start.13 = (bf16[128,1024]{1,0:T(8,128)(2,1)S(1)}, bf16[128,1024]{1,0:T(8,128)(2,1)S(1)}, u32[]{:S(2)}, u32[]{:S(2)}) collective-permute-start(bf16[128,1024]{1,0:T(8,128)(2,1)S(1)} %get-tuple-element.24), channel_id=1, source_target_pairs={{0,24},{8,0},{16,8},{24,16},{1,25},{9,1},{17,9},{25,17},{2,26},{10... | collective-permute-start | bytes 786440 | tf_op jit(solution)/shard_map/ppermute | solution.py:19
  28.4 42.1 %collective-permute-start.2 = (bf16[128,2048]{1,0:T(8,128)(2,1)S(1)}, bf16[128,2048]{1,0:T(8,128)(2,1)S(1)}, u32[]{:S(2)}, u32[]{:S(2)}) collective-permute-start(bf16[128,2048]{1,0:T(8,128)(2,1)S(1)} %pre_grads.2.refs_0_.refs_8_), channel_id=1, source_target_pairs={{0,8},{8,16},{16,24},{1,9},{9,17},{17,25},{2,10},{10,18},{18,26},{... | collective-permute-start | bytes 1572872 | tf_op jit(solution)/shard_map/ppermute | solution.py:29
  38.4 34.0 %collective-permute-start.3 = (bf16[128,2048]{1,0:T(8,128)(2,1)S(1)}, bf16[128,2048]{1,0:T(8,128)(2,1)S(1)}, u32[]{:S(2)}, u32[]{:S(2)}) collective-permute-start(bf16[128,2048]{1,0:T(8,128)(2,1)S(1)} %pre_grads.2.refs_0_.refs_8_), channel_id=1, source_target_pairs={{8,0},{16,8},{24,16},{9,1},{17,9},{25,17},{10,2},{18,10},{26,18},{... | collective-permute-start | bytes 1572872 | tf_op jit(solution)/shard_map/ppermute | solution.py:29
  44.8 23.6 %collective-permute-start.16 = (bf16[128,1024]{1,0:T(8,128)(2,1)S(1)}, bf16[128,1024]{1,0:T(8,128)(2,1)S(1)}, u32[]{:S(2)}, u32[]{:S(2)}) collective-permute-start(bf16[128,1024]{1,0:T(8,128)(2,1)S(1)} %get-tuple-element.29), channel_id=1, source_target_pairs={{0,8},{8,16},{16,24},{24,0},{1,9},{9,17},{17,25},{25,1},{2,10},{10... | collective-permute-start | bytes 786440 | tf_op jit(solution)/shard_map/ppermute | solution.py:19
  65.1 19.3 %collective-permute-start.17 = (bf16[128,1024]{1,0:T(8,128)(2,1)S(1)}, bf16[128,1024]{1,0:T(8,128)(2,1)S(1)}, u32[]{:S(2)}, u32[]{:S(2)}) collective-permute-start(bf16[128,1024]{1,0:T(8,128)(2,1)S(1)} %get-tuple-element.30), channel_id=1, source_target_pairs={{0,16},{8,24},{16,0},{24,8},{1,17},{9,25},{17,1},{25,9},{2,18},{10... | collective-permute-start | bytes 786440 | tf_op jit(solution)/shard_map/ppermute | solution.py:19
  68.5 16.0 %collective-permute-start.18 = (bf16[128,1024]{1,0:T(8,128)(2,1)S(1)}, bf16[128,1024]{1,0:T(8,128)(2,1)S(1)}, u32[]{:S(2)}, u32[]{:S(2)}) collective-permute-start(bf16[128,1024]{1,0:T(8,128)(2,1)S(1)} %get-tuple-element.31), channel_id=1, source_target_pairs={{0,24},{8,0},{16,8},{24,16},{1,25},{9,1},{17,9},{25,17},{2,26},{10... | collective-permute-start | bytes 786440 | tf_op jit(solution)/shard_map/ppermute | solution.py:19
  70.5 18.8 %collective-permute-start.8 = (bf16[128,2048]{1,0:T(8,128)(2,1)S(1)}, bf16[128,2048]{1,0:T(8,128)(2,1)S(1)}, u32[]{:S(2)}, u32[]{:S(2)}) collective-permute-start(bf16[128,2048]{1,0:T(8,128)(2,1)S(1)} %pre_grads.3.refs_1_.refs_9_), channel_id=1, source_target_pairs={{0,8},{8,16},{16,24},{1,9},{9,17},{17,25},{2,10},{10,18},{18,26},{... | collective-permute-start | bytes 1572872 | tf_op jit(solution)/shard_map/ppermute | solution.py:29
  72.4 21.3 %collective-permute-start.9 = (bf16[128,2048]{1,0:T(8,128)(2,1)S(1)}, bf16[128,2048]{1,0:T(8,128)(2,1)S(1)}, u32[]{:S(2)}, u32[]{:S(2)}) collective-permute-start(bf16[128,2048]{1,0:T(8,128)(2,1)S(1)} %pre_grads.3.refs_1_.refs_9_), channel_id=1, source_target_pairs={{8,0},{16,8},{24,16},{9,1},{17,9},{25,17},{10,2},{18,10},{26,18},{... | collective-permute-start | bytes 1572872 | tf_op jit(solution)/shard_map/ppermute | solution.py:29
  76.6 32.1 %collective-permute-start.14 = (bf16[256,2048]{1,0:T(8,128)(2,1)S(1)}, bf16[256,2048]{1,0:T(8,128)(2,1)S(1)}, u32[]{:S(2)}, u32[]{:S(2)}) collective-permute-start(bf16[256,2048]{1,0:T(8,128)(2,1)S(1)} %get-tuple-element.26), channel_id=1, source_target_pairs={{0,1},{1,0},{2,3},{3,2},{4,5},{5,4},{6,7},{7,6},{8,9},{9,8},{10,11... | collective-permute-start | bytes 3145736 | tf_op jit(solution)/shard_map/ppermute | solution.py:19
  84.4 29.5 %collective-permute-start.4 = (bf16[256,2048]{1,0:T(8,128)(2,1)S(1)}, bf16[256,2048]{1,0:T(8,128)(2,1)S(1)}, u32[]{:S(2)}, u32[]{:S(2)}) collective-permute-start(bf16[256,2048]{1,0:T(8,128)(2,1)S(1)} %forward_layer.2), channel_id=1, source_target_pairs={{0,2},{2,4},{4,6},{6,0},{1,3},{3,5},{5,7},{7,1},{8,10},{10,12},{12... | collective-permute-start | bytes 3145736 | tf_op jit(solution)/shard_map/ppermute | solution.py:19
  84.5 29.8 %collective-permute-start.5 = (bf16[256,2048]{1,0:T(8,128)(2,1)S(1)}, bf16[256,2048]{1,0:T(8,128)(2,1)S(1)}, u32[]{:S(2)}, u32[]{:S(2)}) collective-permute-start(bf16[256,2048]{1,0:T(8,128)(2,1)S(1)} %forward_layer.2), channel_id=1, source_target_pairs={{0,3},{1,2},{2,5},{3,4},{4,7},{5,6},{6,1},{7,0},{8,11},{9,10},{10,... | collective-permute-start | bytes 3145736 | tf_op jit(solution)/shard_map/ppermute | solution.py:39
  102.8 21.2 %collective-permute-start.21 = (bf16[128,2048]{1,0:T(8,128)(2,1)S(1)}, bf16[128,2048]{1,0:T(8,128)(2,1)S(1)}, u32[]{:S(2)}, u32[]{:S(2)}) collective-permute-start(bf16[128,2048]{1,0:T(8,128)(2,1)S(1)} %collective-permute-done.8.refs_3_.refs_11_), channel_id=1, source_target_pairs={{0,8},{8,16},{16,24},{1,9},{9,17},{17,25},{2,10},{10,18},{18,26},{... | collective-permute-start | bytes 1572872 | tf_op jit(solution)/shard_map/ppermute | solution.py:29
  106.8 19.1 %collective-permute-start.25 = (bf16[128,2048]{1,0:T(8,128)(2,1)S(1)}, bf16[128,2048]{1,0:T(8,128)(2,1)S(1)}, u32[]{:S(2)}, u32[]{:S(2)}) collective-permute-start(bf16[128,2048]{1,0:T(8,128)(2,1)S(1)} %collective-permute-done.9.refs_4_.refs_21_), channel_id=1, source_target_pairs={{8,0},{16,8},{24,16},{9,1},{17,9},{25,17},{10,2},{18,10},{26,18},{... | collective-permute-start | bytes 1572872 | tf_op jit(solution)/shard_map/ppermute | solution.py:29
  108.7 21.1 %collective-permute-start.22 = (bf16[128,2048]{1,0:T(8,128)(2,1)S(1)}, bf16[128,2048]{1,0:T(8,128)(2,1)S(1)}, u32[]{:S(2)}, u32[]{:S(2)}) collective-permute-start(bf16[128,2048]{1,0:T(8,128)(2,1)S(1)} %collective-permute-done.10.refs_5_.refs_12_), channel_id=1, source_target_pairs={{0,8},{8,16},{16,24},{1,9},{9,17},{17,25},{2,10},{10,18},{18,26},{... | collective-permute-start | bytes 1572872 | tf_op jit(solution)/shard_map/ppermute | solution.py:29
  113.9 43.1 %collective-permute-start.20 = (bf16[256,2048]{1,0:T(8,128)(2,1)S(1)}, bf16[256,2048]{1,0:T(8,128)(2,1)S(1)}, u32[]{:S(2)}, u32[]{:S(2)}) collective-permute-start(bf16[256,2048]{1,0:T(8,128)(2,1)S(1)} %input_grads.1.refs_7_), channel_id=1, source_target_pairs={{0,6},{2,0},{4,2},{6,4},{1,7},{3,1},{5,3},{7,5},{8,14},{10,8},{12,... | collective-permute-start | bytes 3145736 | tf_op jit(solution)/shard_map/ppermute | solution.py:19
  121.5 35.5 %collective-permute-start.19 = (bf16[256,2048]{1,0:T(8,128)(2,1)S(1)}, bf16[256,2048]{1,0:T(8,128)(2,1)S(1)}, u32[]{:S(2)}, u32[]{:S(2)}) collective-permute-start(bf16[256,2048]{1,0:T(8,128)(2,1)S(1)} %forward_layer.3.refs_22_), channel_id=1, source_target_pairs={{0,6},{2,0},{4,2},{6,4},{1,7},{3,1},{5,3},{7,5},{8,14},{10,8},{12,... | collective-permute-start | bytes 3145736 | tf_op jit(solution)/shard_map/ppermute | solution.py:19
  124.0 16.7 %collective-permute-start.24 = (bf16[128,2048]{1,0:T(8,128)(2,1)S(1)}, bf16[128,2048]{1,0:T(8,128)(2,1)S(1)}, u32[]{:S(2)}, u32[]{:S(2)}) collective-permute-start(bf16[128,2048]{1,0:T(8,128)(2,1)S(1)} %collective-permute-done.11.refs_6_.refs_18_), channel_id=1, source_target_pairs={{8,0},{16,8},{24,16},{9,1},{17,9},{25,17},{10,2},{18,10},{26,18},{... | collective-permute-start | bytes 1572872 | tf_op jit(solution)/shard_map/ppermute | solution.py:29
  125.9 14.8 %collective-permute-start.23 = (bf16[128,2048]{1,0:T(8,128)(2,1)S(1)}, bf16[128,2048]{1,0:T(8,128)(2,1)S(1)}, u32[]{:S(2)}, u32[]{:S(2)}) collective-permute-start(bf16[128,2048]{1,0:T(8,128)(2,1)S(1)} %collective-permute-done.21.refs_13_), channel_id=1, source_target_pairs={{0,8},{8,16},{16,24},{1,9},{9,17},{17,25},{2,10},{10,18},{18,26},{... | collective-permute-start | bytes 1572872 | tf_op jit(solution)/shard_map/ppermute | solution.py:29
  129.9 20.0 %collective-permute-start.26 = (bf16[128,2048]{1,0:T(8,128)(2,1)S(1)}, bf16[128,2048]{1,0:T(8,128)(2,1)S(1)}, u32[]{:S(2)}, u32[]{:S(2)}) collective-permute-start(bf16[128,2048]{1,0:T(8,128)(2,1)S(1)} %collective-permute-done.25.refs_19_), channel_id=1, source_target_pairs={{8,0},{16,8},{24,16},{9,1},{17,9},{25,17},{10,2},{18,10},{26,18},{... | collective-permute-start | bytes 1572872 | tf_op jit(solution)/shard_map/ppermute | solution.py:29
  (7 other events, 64.1 us)

commit v3 on v1

v3 whole, which is shorter than its diff:
```python
import functools

import jax
import jax.numpy as jnp
from jax import lax
from jax.experimental import pallas as pl
from jax.experimental.pallas import tpu as pltpu
from jax.sharding import PartitionSpec as P

EPS = 1e-05
BF16 = jnp.bfloat16
F32 = jnp.float32
VMEM_LIMIT = 12 * 2**20


def shift(value, axis, steps):
    count = lax.axis_size(axis)
    return lax.ppermute(value, axis, [(at, (at + steps) % count) for at in range(count)])


def swap(value, axis):
    return shift(value, axis, 1)


def along(value, axis, steps, skipped=0):
    count = lax.axis_size(axis)
    held = range(skipped, count) if steps > 0 else range(count - skipped)
    pairs = [(at, at + steps) for at in held if 0 <= at + steps < count]
    return lax.ppermute(value, axis, pairs)


def across(value, axis, steps):
    count = lax.axis_size(axis)
    pairs = [(at, at + steps) for at in range(count - steps)]
    return lax.ppermute(value, axis, pairs + [(target, source) for source, target in pairs])


def shift_and_swap(value, steps):
    sections, halves = lax.axis_size("section"), lax.axis_size("mp")
    pairs = [
        (at * halves + half, ((at + steps) % sections) * halves + (half + 1) % halves)
        for at in range(sections)
        for half in range(halves)
    ]
    return lax.ppermute(value, ("section", "mp"), pairs)


VMEM = pl.BlockSpec(memory_space=pltpu.VMEM)
SMEM = pl.BlockSpec(memory_space=pltpu.SMEM)
ANY = pl.BlockSpec(memory_space=pl.ANY)


def call(kernel, name, place, values, outs, tokens=(), scratch=(), limit=VMEM_LIMIT, flops=1000):
    counted = len(values)

    def run(place_ref, *refs):
        kernel(place_ref, *refs[:counted], *refs[counted + len(tokens) :])

    return pl.pallas_call(
        run,
        in_specs=[SMEM] + [VMEM] * len(values) + [ANY] * len(tokens),
        out_specs=[VMEM] * len(outs),
        out_shape=outs,
        scratch_shapes=scratch,
        compiler_params=pltpu.CompilerParams(vmem_limit_bytes=limit),
        cost_estimate=pl.CostEstimate(flops=flops, bytes_accessed=1000, transcendentals=0),
        name=name,
    )(place, *values, *tokens)


def array(*shape):
    dtype = shape[-1] if shape[-1] is F32 else BF16
    return jax.ShapeDtypeStruct(tuple(size for size in shape if size is not F32), dtype)


def gelu(v):
    scale = 0.7978845608028654
    return 0.5 * v * (1.0 + jnp.tanh(scale * (v + 0.044715 * (v * v * v))))


def gelu_slope(v):
    scale = 0.7978845608028654
    square = v * v
    t = jnp.tanh(scale * (v + 0.044715 * (square * v)))
    return 0.5 * (1.0 + t) + 0.5 * v * (1.0 - t * t) * (scale * (1.0 + 3 * 0.044715 * square))


def normalize_into(own_ref, other_ref, normed_ref, half, own_start=0, step=128):
    rows, columns = other_ref.shape
    own_at = pl.multiple_of(half * columns, columns)
    other_at = pl.multiple_of((1 - half) * columns, columns)
    inverses = []
    for start in range(0, rows, step):
        at = slice(start, start + step)
        own = own_ref[own_start + start : own_start + start + step, :].astype(F32)
        other = other_ref[at, :].astype(F32)
        total = jnp.sum(own, axis=-1, keepdims=True) + jnp.sum(other, axis=-1, keepdims=True)
        average = total / (2 * columns)
        own, other = own - average, other - average
        total = jnp.sum(own * own, axis=-1, keepdims=True)
        total = total + jnp.sum(other * other, axis=-1, keepdims=True)
        inverse = lax.rsqrt(total / (2 * columns) + EPS)
        normed_ref[at, pl.ds(own_at, columns)] = (own * inverse).astype(BF16)
        normed_ref[at, pl.ds(other_at, columns)] = (other * inverse).astype(BF16)
        inverses.append(inverse)
    return inverses


def split_blocks(place_ref, normed_ref, rows, block_refs, replicas, first=0):
    block = block_refs[0].shape[1]
    for steps in range(first, len(block_refs)):
        target = lax.rem(place_ref[0] + steps, replicas)
        block_refs[steps][...] = normed_ref[rows, pl.ds(pl.multiple_of(target * block, block), block)]


def norm_kernel(place_ref, own_ref, other_ref, normed_ref, inverse_ref, scaled_ref, *block_refs):
    rows, columns = own_ref.shape
    half = place_ref[1]
    for index, inverse in enumerate(normalize_into(own_ref, other_ref, normed_ref, half)):
        at = slice(index * 128, (index + 1) * 128)
        inverse_ref[at, :] = jnp.broadcast_to(inverse, (128, inverse_ref.shape[1]))
    scaled_ref[...] = normed_ref[:, pl.ds(pl.multiple_of(half * columns, columns), columns)]
    part = rows // 2
    split_blocks(place_ref, normed_ref, slice(None), block_refs[:1], len(block_refs))
    mine = pl.ds(pl.multiple_of(half * part, part), part)
    split_blocks(place_ref, normed_ref, mine, block_refs, len(block_refs), 1)


def norm_rows(place, own, other, replicas, tokens=()):
    rows, columns = own.shape
    block = 2 * columns // replicas
    outs = [array(rows, 2 * columns), array(rows, 128, F32), array(rows, columns), array(rows, block)]
    outs += [array(rows // 2, block)] * (replicas - 1)
    return call(norm_kernel, "norm_rows", place, [own, other], outs, tokens)


def backward_kernel(
    place_ref, normed_ref, weight_ref, cot_ref, grad_ref, send_ref, keep_ref, sums_ref, tile=512
):
    rows, columns = cot_ref.shape
    half = place_ref[1]
    for start in range(0, columns, tile):
        at = slice(start, start + tile)
        preact = jnp.dot(normed_ref[...], weight_ref[:, at], preferred_element_type=F32)
        grad_ref[:, at] = (cot_ref[:, at].astype(F32) * gelu_slope(preact)).astype(BF16)
    first = jnp.zeros((rows, 1), F32)
    second = jnp.zeros((rows, 1), F32)
    for is_mine in (False, True):
        at_half = half if is_mine else 1 - half
        for start in range(0, columns, tile):
            features = pl.ds(pl.multiple_of(at_half * columns + start, tile), tile)
            part = lax.dot_general(
                grad_ref[...], weight_ref[features, :], (((1,), (1,)), ((), ())), preferred_element_type=F32
            )
            first += jnp.sum(part, axis=-1, keepdims=True)
            second += jnp.sum(part * normed_ref[:, features].astype(F32), axis=-1, keepdims=True)
            if is_mine:
                keep_ref[:, start : start + tile] = part
            else:
                send_ref[:, start : start + tile] = part.astype(BF16)
    lane = lax.broadcasted_iota(jnp.int32, (rows, 128), 1)
    left = jnp.where(lane < 64, first, second)
    sums_ref[...] = left
    terms = jnp.zeros((rows, 128), F32)
    for index in range(3):
        term = left.astype(BF16).astype(F32)
        left = left - term
        terms = jnp.where(lane % 64 // 16 == index, term, terms)
    send_ref[:, columns : columns + 128] = terms.astype(BF16)


def backward_rows(place, normed, weight, cot, tokens=()):
    rows, columns = cot.shape
    outs = [array(rows, columns), array(rows, columns + 128), array(rows, columns, F32), array(rows, 128, F32)]
    return call(backward_kernel, "backward_rows", place, [normed, weight, cot], outs, tokens)


def stack_kernel(place_ref, *refs):
    rows = refs[0].shape[0]
    for index, ref in enumerate(refs[:-1]):
        refs[-1][index * rows : (index + 1) * rows, :] = ref[...]


def stack(place, values, tokens=()):
    rows, columns = values[0].shape
    return call(stack_kernel, "stack_blocks", place, values, [array(len(values) * rows, columns)], tokens)[0]


def load_kernel(place_ref, weight_ref, held_ref, sem):
    copy = pltpu.make_async_copy(weight_ref, held_ref, sem)
    copy.start()
    copy.wait()


def load(place, weight):
    held = pl.pallas_call(
        load_kernel,
        in_specs=[SMEM, ANY],
        out_specs=VMEM,
        out_shape=pltpu.VMEM(weight.shape, weight.dtype),
        scratch_shapes=[pltpu.SemaphoreType.DMA],
        compiler_params=pltpu.CompilerParams(vmem_limit_bytes=VMEM_LIMIT),
        name="load_weights",
    )(place, weight)
    return pltpu.with_memory_space_constraint(held, pltpu.VMEM)


def forward_kernel(place_ref, own_ref, other_ref, weight_ref, out_ref, normed_ref, tile=256):
    normalize_into(own_ref, other_ref, normed_ref, place_ref[1])
    for start in range(0, out_ref.shape[1], tile):
        at = slice(start, start + tile)
        preact = jnp.dot(normed_ref[...], weight_ref[:, at], preferred_element_type=F32)
        out_ref[:, at] = (own_ref[:, at].astype(F32) + gelu(preact)).astype(BF16)


def forward_layer(place, own, other, weight, tokens=()):
    scratch = [pltpu.VMEM((own.shape[0], weight.shape[0]), BF16)]
    return call(
        forward_kernel, "forward_layer", place, [own, other, weight], [array(*own.shape)], tokens, scratch
    )[0]


def input_grad_kernel(
    place_ref, cot_ref, keep_ref, arrived_ref, sums_ref, inverse_ref, scaled_ref, out_ref
):
    columns = cot_ref.shape[1]
    depth = 2 * columns
    terms = arrived_ref[:, columns : columns + 128].astype(F32)
    first = sums_ref[:, 0:1] + ((terms[:, 0:1] + terms[:, 16:17]) + terms[:, 32:33])
    second = sums_ref[:, 64:65] + ((terms[:, 64:65] + terms[:, 80:81]) + terms[:, 96:97])
    dnormed = keep_ref[...] + arrived_ref[:, :columns].astype(F32)
    scaled = scaled_ref[...].astype(F32)
    out_ref[...] = (
        cot_ref[...].astype(F32)
        + inverse_ref[:, 0:1] * (dnormed - first / depth - scaled * (second / depth))
    ).astype(BF16)


def input_grads(place, cot, keep, arrived, sums, inverse, scaled, tokens=()):
    values = [cot, keep, arrived, sums, inverse, scaled]
    return call(input_grad_kernel, "input_grads", place, values, [array(*cot.shape)], tokens)[0]


def gather_kernel(replicas, place_ref, own_ref, *refs):
    near_refs, (far_ref, out_ref, blocks) = refs[: replicas - 1], refs[replicas - 1 :]
    rows = own_ref.shape[0]
    part = rows // 2
    half = place_ref[1]
    blocks[:rows, :] = own_ref[...]
    for steps in range(1, replicas):
        near = pl.ds(pl.multiple_of(rows * steps + half * part, part), part)
        far = pl.ds(pl.multiple_of(rows * steps + (1 - half) * part, part), part)
        blocks[near, :] = near_refs[steps - 1][...]
        blocks[far, :] = far_ref[(steps - 1) * part : steps * part, :]
    out_ref[...] = blocks[...].T


def gather_blocks(place, own, near, far):
    replicas = len(near) + 1
    rows, block = own.shape
    kernel = functools.partial(gather_kernel, replicas)
    scratch = [pltpu.VMEM((replicas * rows, block), BF16)]
    outs = [array(block, replicas * rows)]
    return call(
        kernel, "gather_blocks", place, [own, *near, far], outs, (), scratch
    )[0]


def gather_grad_kernel(place_ref, own_ref, *refs):
    *refs, out_ref = refs
    others = len(refs) // 2
    rows = own_ref.shape[0]
    out_ref[:rows, :] = own_ref[...]
    for steps in range(1, others + 1):
        out_ref[rows * steps : rows * (steps + 1), :] = jnp.where(
            place_ref[0] >= steps, refs[steps - 1][...], refs[others + steps - 1][...]
        )


def gather_grads(place, own, ups, downs):
    values = [own, *ups, *downs]
    outs = [array((len(ups) + 1) * own.shape[0], own.shape[1])]
    return call(
        gather_grad_kernel, "gather_grads", place, values, outs, limit=16 * 2**20, flops=3 * 10**10
    )[0]


def weight_grad_kernel(passed, place_ref, *refs, width=512):
    blocks_ref, grads_ref, *refs = refs
    pass_refs, out_ref, pass_outs = refs[:passed], refs[passed], refs[passed + 1 : 2 * passed + 1]
    held, sems, pass_sems = refs[-3:]
    passing = [
        pltpu.make_async_copy(pass_refs[at], pass_outs[at], pass_sems.at[at]) for at in range(passed)
    ]
    for copy in passing:
        copy.start()
    stores = []
    for index, start in enumerate(range(0, grads_ref.shape[1], width)):
        at = slice(start, start + width)
        held[:, at] = jnp.dot(
            blocks_ref[...], grads_ref[:, at], preferred_element_type=F32
        ).astype(BF16)
        stores.append(pltpu.make_async_copy(held.at[:, at], out_ref.at[:, at], sems.at[index]))
        stores[-1].start()
    for copy in stores + passing:
        copy.wait()


def weight_grads(place, blocks, grads, passes, width=512, limit=20 * 2**20):
    block, columns = blocks.shape[0], grads.shape[1]
    outs = [array(block, columns)] + [array(*value.shape) for value in passes]
    return pl.pallas_call(
        functools.partial(weight_grad_kernel, len(passes), width=width),
        in_specs=[SMEM] + [VMEM] * (2 + len(passes)),
        out_specs=[ANY] * len(outs),
        out_shape=outs,
        scratch_shapes=[
            pltpu.VMEM((block, columns), BF16),
            pltpu.SemaphoreType.DMA((columns // width,)),
            pltpu.SemaphoreType.DMA((len(passes),)),
        ],
        compiler_params=pltpu.CompilerParams(vmem_limit_bytes=limit),
        cost_estimate=pl.CostEstimate(flops=1000, bytes_accessed=1000, transcendentals=0),
        name="weight_grads",
    )(place, blocks, grads, *passes)


def after(value, *others):
    return lax.optimization_barrier((value, *others))[0]


def body(act_in, weights, act_saved, cotangent):
    weight = weights[0]
    own_in, own_saved, own_cot = act_in[0], act_saved[0], cotangent[0]
    replicas = lax.axis_size("dp")
    place = jnp.stack([lax.axis_index("dp"), lax.axis_index("mp")]).astype(jnp.int32)

    other_saved = swap(own_saved, "mp")
    weight = load(place, weight)
    other_in = swap(after(own_in, weight), "mp")

    normed, inverse, scaled, own_block, *blocks = norm_rows(
        place, own_saved, other_saved, replicas, [weight]
    )
    near = [shift(block, "dp", steps + 1) for steps, block in enumerate(blocks)]
    grad, send, keep, sums = backward_rows(place, normed, weight, own_cot)

    grad = after(grad, *near)
    arrived = swap(after(send, other_in, *near), "mp")
    ups, downs = [grad], [grad]
    for steps in range(1, replicas):
        if steps <= replicas // 2:
            ups.append(along(ups[-1], "dp", 1, steps - 1))
            downs.append(along(downs[-1], "dp", -1, steps - 1))
        else:
            ups.append(across(after(grad, ups[1], downs[1]), "dp", steps))
            downs.append(ups[-1])

    forward = forward_layer(place, own_in, other_in, weight)
    received = shift(after(forward, *near), "section", 1)
    received_other = shift_and_swap(after(forward, arrived), 1)

    far = swap(after(stack(place, near), received_other), "mp")
    shadow_there = forward_layer(place, received, received_other, weight)
    shadow = shift(shadow_there, "section", -1)

    input_grad = input_grads(place, own_cot, keep, arrived, sums, inverse, scaled)
    grad_back = shift(after(input_grad, received_other), "section", -1)

    weight_grad, received, shadow, grad_back = weight_grads(
        place,
        gather_blocks(place, own_block, near, far),
        gather_grads(place, grad, ups[1:], downs[:0:-1]),
        [received, shadow, grad_back],
    )
    return (received[None], shadow[None], grad_back[None], weight_grad[None])


def solution(mesh):
    return jax.shard_map(
        body,
        mesh=mesh,
        in_specs=(
            P("section", "dp", "mp"),
            P("section", None, "mp"),
            P("section", "dp", "mp"),
            P("section", "dp", "mp"),
        ),
        out_specs=(
            P("section", "dp", "mp"),
            P("section", "dp", "mp"),
            P("section", "dp", "mp"),
            P("section", "dp", "mp"),
        ),
        check_vma=False,
    )
```

time: 281 us -> 142 us (0.51)
  waiting for transfers between devices: 169 us -> 66.7 us
  matrix products: 52.8 us -> 0 us
  Pallas kernels: 0 us -> 38.5 us
  other arithmetic: 15.7 us -> 0.07 us
  local copies, waits for them, and re-layouts: 9.92 us -> 5.78 us
  starting transfers between devices: 32.2 us -> 28.7 us
    ppermute x6 -> x5, waiting for transfers between devices: 90 us -> 18 us  [the longest x4 18 us: along(): return lax.ppermute(value, axis, pairs)]
    dot_general x5 -> x0, matrix products: 52.8 us -> none  [the longest x2 22.7 us: forward_layer(): preact = jnp.dot(normed, weight, preferred_element_type=jnp.float32)]
    pallas_call x0 -> x10, Pallas kernels: none -> 38.5 us  [the longest x8 30.7 us: call(): pl.pallas_call(run, in_specs=[SMEM] + [VMEM] * len(values) + [ANY] * len(...]
    ppermute x10, waiting for transfers between devices: 64.9 us -> 38.6 us  [shift(): lax.ppermute(value, axis, [(at, (at + steps) % count) for at in range(cou...]
    select_n x5 -> x0, other arithmetic: 6.64 us -> none  [the longest x2 3.81 us: whole_rows(): jnp.where(first, own, other)]
    convert_element_type x2 -> x0, other arithmetic: 5.82 us -> none  [the longest x1 4.97 us: body(): pre_grad = pullback(own_cot.astype(jnp.float32))[0].astype(jnp.bfloat16)]
    ppermute x6 -> x5, starting transfers between devices: 19.2 us -> 14.1 us  [the longest x4 13.4 us: along(): return lax.ppermute(value, axis, pairs)]
    ppermute x10, starting transfers between devices: 10.2 us -> 14.4 us  [shift(): lax.ppermute(value, axis, [(at, (at + steps) % count) for at in range(cou...]
  transfers between devices with their start and end apart: 17 -> 16, of which waited for: 11 -> 9; matrix products, arithmetic and copies ran while one was open for 11% -> 0% of each run, Pallas kernels for 0% -> 23%
where the time goes in v3:
time: 142 us; the launch traced here: 141 us
  waiting for transfers between devices  66.7 us (47%)
  Pallas kernels  38.5 us (27%)
  starting transfers between devices  28.7 us (20%)
  local copies, waits for them, and re-layouts  5.78 us (4%)
    ppermute x10, waiting for transfers between devices, shift(): lax.ppermute(value, axis, [(at, (at + steps) % count) for at in range(cou...  38.6 us
    pallas_call x8, Pallas kernels, call(): pl.pallas_call(run, in_specs=[SMEM] + [VMEM] * len(values) + [ANY] * len(...  30.7 us
    ppermute x4, waiting for transfers between devices, along(): return lax.ppermute(value, axis, pairs)  18 us
    ppermute x10, starting transfers between devices, shift(): lax.ppermute(value, axis, [(at, (at + steps) % count) for at in range(cou...  14.4 us
    ppermute x4, starting transfers between devices, along(): return lax.ppermute(value, axis, pairs)  13.4 us
    ppermute x1, waiting for transfers between devices, shift_and_swap(): return lax.ppermute(value, ('section', 'mp'), pairs)  10.1 us
    pallas_call x1, Pallas kernels, weight_grads(): pl.pallas_call(functools.partial(weight_grad_kernel, len(passes), width=w...  6.08 us
    unnamed x8, local copies, waits for them, and re-layouts  5.78 us
  transfers between devices with their start and end apart: 16, of which 9 were waited for; matrix products, arithmetic and copies ran while one was open for 0% of the time, Pallas kernels for 23%

profile of v3, /device:TPU:8, one launch (start us, length us, event | category | flops | bytes accessed | tf_op | source)
XLA Modules:
  0.0 140.8 jit_solution(16426046070295085334)
XLA Ops:
  0.6 1.6 %collective-permute-start = (bf16[256,2048]{1,0:T(8,128)(2,1)}, bf16[256,2048]{1,0:T(8,128)(2,1)S(1)}, u32[]{:S(2)}, u32[]{:S(2)}) collective-permute-start(bf16[256,2048]{1,0:T(8,128)(2,1)} %bitcast.15), channel_id=1, source_target_pairs={{0,1},{1,0},{2,3},{3,2},{4,5},{5,4},{6,7},{7,6},{8,9},{9,8},{10,11... | collective-permute-start | bytes 3145736 | tf_op jit(solution)/shard_map/ppermute | solution.py:18
  2.3 5.8 %copy-done = bf16[1,4096,2048]{2,1,0:T(8,128)(2,1)S(1)} copy-done((bf16[1,4096,2048]{2,1,0:T(8,128)(2,1)S(1)}, bf16[1,4096,2048]{2,1,0:T(8,128)(2,1)}, u32[]{:S(2)}) %copy-start) | copy-done | bytes 16777240
  8.1 1.7 %load_weights.1.refs_2_.refs_1_ = bf16[4096,2048]{1,0:T(8,128)(2,1)S(1)} custom-call(s32[2]{0:T(128)S(1)} %pad_add_fusion.place_ref, bf16[4096,2048]{1,0:T(8,128)(2,1)S(1)} %bitcast.10), custom_call_target="tpu_custom_call" | custom-call | tf_op jit(solution)/shard_map/load_weights/pallas_call | solution.py:196
  10.4 16.6 %collective-permute-done.refs_1_ = bf16[256,2048]{1,0:T(8,128)(2,1)S(1)} collective-permute-done((bf16[256,2048]{1,0:T(8,128)(2,1)}, bf16[256,2048]{1,0:T(8,128)(2,1)S(1)}, u32[]{:S(2)}, u32[]{:S(2)}) %collective-permute-start) | collective-permute-done | bytes 1048608 | tf_op jit(solution)/shard_map/ppermute | solution.py:18
  27.0 2.0 %norm_rows.1 = (bf16[256,4096]{1,0:T(8,128)(2,1)S(1)}, f32[256,128]{1,0:T(8,128)S(1)}, bf16[256,2048]{1,0:T(8,128)(2,1)S(1)}, bf16[256,1024]{1,0:T(8,128)(2,1)S(...) custom-call(s32[2]{0:T(128)S(1)} %pad_add_fusion.place_ref, ...), custom_call_target="tpu_custom_call" | custom-call | flops 1000 | bytes 1000 | tf_op jit(solution)/shard_map/norm_rows/pallas_call | solution.py:59
  29.0 1.6 %collective-permute-start.1 = (bf16[128,1024]{1,0:T(8,128)(2,1)S(1)}, bf16[128,1024]{1,0:T(8,128)(2,1)S(1)}, u32[]{:S(2)}, u32[]{:S(2)}) collective-permute-start(bf16[128,1024]{1,0:T(8,128)(2,1)S(1)} %get-tuple-element.28), channel_id=1, source_target_pairs={{0,8},{8,16},{16,24},{24,0},{1,9},{9,17},{17,25},{25,1},{2,10},{10... | collective-permute-start | bytes 786440 | tf_op jit(solution)/shard_map/ppermute | solution.py:18
  31.7 1.9 %collective-permute-start.3 = (bf16[128,1024]{1,0:T(8,128)(2,1)S(1)}, bf16[128,1024]{1,0:T(8,128)(2,1)S(1)}, u32[]{:S(2)}, u32[]{:S(2)}) collective-permute-start(bf16[128,1024]{1,0:T(8,128)(2,1)S(1)} %get-tuple-element.30), channel_id=1, source_target_pairs={{0,24},{8,0},{16,8},{24,16},{1,25},{9,1},{17,9},{25,17},{2,26},{10... | collective-permute-start | bytes 786440 | tf_op jit(solution)/shard_map/ppermute | solution.py:18
  33.6 10.2 %backward_rows.1 = (bf16[256,2048]{1,0:T(8,128)(2,1)S(1)}, bf16[256,2176]{1,0:T(8,128)(2,1)S(1)}, f32[256,2048]{1,0:T(8,128)S(1)}, f32[256,128]{1,0:T(8,128)S(1)}) custom-call(s32[2]{0:T(128)S(1)} %pad_add_fusion.place_ref, bf16[256,4096]{1,0:T(8,128)(2,1)S(1)} %get-tuple-element.32.refs_0_, bf16[4096,2048]{1,0:T(8,128)(2,1)S(1)} %load_weights.1.refs_2_.refs_1_, ...), custom_call_target="tpu_custom_call" | custom-call | flops 1000 | bytes 1000 | tf_op jit(solution)/shard_map/backward_rows/pallas_call | solution.py:59
  43.8 4.5 %collective-permute-done.4.refs_1_ = bf16[256,2048]{1,0:T(8,128)(2,1)S(1)} collective-permute-done((bf16[256,2048]{1,0:T(8,128)(2,1)S(1)}, bf16[256,2048]{1,0:T(8,128)(2,1)S(1)}, u32[]{:S(2)}, u32[]{:S(2)}) %collective-permute-start.4) | collective-permute-done | bytes 1048608 | tf_op jit(solution)/shard_map/ppermute | solution.py:18
  48.3 2.7 %collective-permute-done.2.refs_1_.refs_2_ = bf16[128,1024]{1,0:T(8,128)(2,1)S(1)} collective-permute-done((bf16[128,1024]{1,0:T(8,128)(2,1)S(1)}, bf16[128,1024]{1,0:T(8,128)(2,1)S(1)}, u32[]{:S(2)}, u32[]{:S(2)}) %collective-permute-start.2) | collective-permute-done | bytes 262176 | tf_op jit(solution)/shard_map/ppermute | solution.py:18
  51.0 1.8 %collective-permute-done.3.refs_2_.refs_3_ = bf16[128,1024]{1,0:T(8,128)(2,1)S(1)} collective-permute-done((bf16[128,1024]{1,0:T(8,128)(2,1)S(1)}, bf16[128,1024]{1,0:T(8,128)(2,1)S(1)}, u32[]{:S(2)}, u32[]{:S(2)}) %collective-permute-start.3) | collective-permute-done | bytes 262176 | tf_op jit(solution)/shard_map/ppermute | solution.py:18
  52.8 1.5 %collective-permute-start.5 = (bf16[256,2176]{1,0:T(8,128)(2,1)S(1)}, bf16[256,2176]{1,0:T(8,128)(2,1)S(1)}, u32[]{:S(2)}, u32[]{:S(2)}) collective-permute-start(bf16[256,2176]{1,0:T(8,128)(2,1)S(1)} %get-tuple-element.34), channel_id=1, source_target_pairs={{0,1},{1,0},{2,3},{3,2},{4,5},{5,4},{6,7},{7,6},{8,9},{9,8},{10,11... | collective-permute-start | bytes 3342344 | tf_op jit(solution)/shard_map/ppermute | solution.py:18
  54.3 1.9 %collective-permute-start.10 = (bf16[256,2048]{1,0:T(8,128)(2,1)S(1)}, bf16[256,2048]{1,0:T(8,128)(2,1)S(1)}, u32[]{:S(2)}, u32[]{:S(2)}) collective-permute-start(bf16[256,2048]{1,0:T(8,128)(2,1)S(1)} %get-tuple-element.39.refs_0_), channel_id=1, source_target_pairs={{8,0},{16,8},{24,16},{9,1},{17,9},{25,17},{10,2},{18,10},{26,18},{... | collective-permute-start | bytes 3145736 | tf_op jit(solution)/shard_map/ppermute | solution.py:29
  56.2 4.1 %collective-permute-start.8 = (bf16[256,2048]{1,0:T(8,128)(2,1)S(1)}, bf16[256,2048]{1,0:T(8,128)(2,1)S(1)}, u32[]{:S(2)}, u32[]{:S(2)}) collective-permute-start(bf16[256,2048]{1,0:T(8,128)(2,1)S(1)} %get-tuple-element.39.refs_0_), channel_id=1, source_target_pairs={{0,8},{8,16},{16,24},{1,9},{9,17},{17,25},{2,10},{10,18},{18,26},{... | collective-permute-start | bytes 3145736 | tf_op jit(solution)/shard_map/ppermute | solution.py:29
  60.3 7.2 %forward_layer.2 = bf16[256,2048]{1,0:T(8,128)(2,1)S(1)} custom-call(s32[2]{0:T(128)S(1)} %pad_add_fusion.place_ref, bf16[256,2048]{1,0:T(8,128)(2,1)S(1)} %bitcast.14, bf16[256,2048]{1,0:T(8,128)(2,1)S(1)} %collective-permute-done.4.refs_1_, bf16[4096,2048]{1,0:T(8,128)(2,1)S(1)} %load_weights.1.refs_2_.refs_1_), custom_call_target="tpu_custom_call" | custom-call | flops 1000 | bytes 1000 | tf_op jit(solution)/shard_map/forward_layer/pallas_call | solution.py:59
  67.5 11.8 %collective-permute-done.5.refs_2_ = bf16[256,2176]{1,0:T(8,128)(2,1)S(1)} collective-permute-done((bf16[256,2176]{1,0:T(8,128)(2,1)S(1)}, bf16[256,2176]{1,0:T(8,128)(2,1)S(1)}, u32[]{:S(2)}, u32[]{:S(2)}) %collective-permute-start.5) | collective-permute-done | bytes 1114144 | tf_op jit(solution)/shard_map/ppermute | solution.py:18
  79.5 2.3 %collective-permute-start.13 = (bf16[256,2048]{1,0:T(8,128)(2,1)S(1)}, bf16[256,2048]{1,0:T(8,128)(2,1)S(1)}, u32[]{:S(2)}, u32[]{:S(2)}) collective-permute-start(bf16[256,2048]{1,0:T(8,128)(2,1)S(1)} %forward_layer.2), channel_id=1, source_target_pairs={{0,2},{2,4},{4,6},{6,0},{1,3},{3,5},{5,7},{7,1},{8,10},{10,12},{12... | collective-permute-start | bytes 3145736 | tf_op jit(solution)/shard_map/ppermute | solution.py:18
  83.6 6.0 %collective-permute-start.12 = (bf16[256,2048]{1,0:T(8,128)(2,1)S(1)}, bf16[256,2048]{1,0:T(8,128)(2,1)S(1)}, u32[]{:S(2)}, u32[]{:S(2)}) collective-permute-start(bf16[256,2048]{1,0:T(8,128)(2,1)S(1)} %collective-permute-done.10.refs_6_), channel_id=1, source_target_pairs={{8,0},{16,8},{9,1},{17,9},{10,2},{18,10},{11,3},{19,11},{12,4},{20... | collective-permute-start | bytes 3145736 | tf_op jit(solution)/shard_map/ppermute | solution.py:29
  89.6 1.4 collective-permute-start.9
  92.9 10.1 %collective-permute-done.6.refs_1_ = bf16[256,2048]{1,0:T(8,128)(2,1)S(1)} collective-permute-done((bf16[256,2048]{1,0:T(8,128)(2,1)S(1)}, bf16[256,2048]{1,0:T(8,128)(2,1)S(1)}, u32[]{:S(2)}, u32[]{:S(2)}) %collective-permute-start.6) | collective-permute-done | bytes 1048608 | tf_op jit(solution)/shard_map/ppermute | solution.py:45
  103.1 2.9 %collective-permute-start.15 = (bf16[256,2048]{1,0:T(8,128)(2,1)S(1)}, bf16[256,2048]{1,0:T(8,128)(2,1)S(1)}, u32[]{:S(2)}, u32[]{:S(2)}) collective-permute-start(bf16[256,2048]{1,0:T(8,128)(2,1)S(1)} %input_grads.1), channel_id=1, source_target_pairs={{0,6},{2,0},{4,2},{6,4},{1,7},{3,1},{5,3},{7,5},{8,14},{10,8},{12,... | collective-permute-start | bytes 3145736 | tf_op jit(solution)/shard_map/ppermute | solution.py:18
  106.0 7.2 %forward_layer.3 = bf16[256,2048]{1,0:T(8,128)(2,1)S(1)} custom-call(s32[2]{0:T(128)S(1)} %pad_add_fusion.place_ref, bf16[256,2048]{1,0:T(8,128)(2,1)S(1)} %collective-permute-done.13.refs_0_.refs_2_, bf16[256,2048]{1,0:T(8,128)(2,1)S(1)} %collective-permute-done.6.refs_1_, bf16[4096,2048]{1,0:T(8,128)(2,1)S(1)} %load_weights.1.refs_2_.refs_1_), custom_call_target="tpu_custom_call" | custom-call | flops 1000 | bytes 1000 | tf_op jit(solution)/shard_map/forward_layer/pallas_call | solution.py:59
  114.1 16.9 %collective-permute-done.12.refs_5_ = bf16[256,2048]{1,0:T(8,128)(2,1)S(1)} collective-permute-done((bf16[256,2048]{1,0:T(8,128)(2,1)S(1)}, bf16[256,2048]{1,0:T(8,128)(2,1)S(1)}, u32[]{:S(2)}, u32[]{:S(2)}) %collective-permute-start.12) | collective-permute-done | bytes 1048608 | tf_op jit(solution)/shard_map/ppermute | solution.py:29
  134.6 6.1 %weight_grads.1 = (bf16[1024,2048]{1,0:T(8,128)(2,1)}, bf16[256,2048]{1,0:T(8,128)(2,1)}, bf16[256,2048]{1,0:T(8,128)(2,1)}, bf16[256,2048]{1,0:T(8,128)(2,1)}) custom-call(s32[2]{0:T(128)S(1)} %pad_add_fusion.place_ref, bf16[1024,1024]{1,0:T(8,128)(2,1)S(1)} %gather_blocks.1.refs_0_, bf16[1024,2048]{1,0:T(8,128)(2,1)S(1)} %gather_grads.1.refs_1_, ...), custom_call_target="tpu_custom_call" | custom-call | flops 1000 | bytes 1000 | tf_op jit(solution)/shard_map/weight_grads/pallas_call | solution.py:312
  (27 shorter events, 10.2 us)
Async XLA Ops:
  0.6 26.3 %collective-permute-start = (bf16[256,2048]{1,0:T(8,128)(2,1)}, bf16[256,2048]{1,0:T(8,128)(2,1)S(1)}, u32[]{:S(2)}, u32[]{:S(2)}) collective-permute-start(bf16[256,2048]{1,0:T(8,128)(2,1)} %bitcast.15), channel_id=1, source_target_pairs={{0,1},{1,0},{2,3},{3,2},{4,5},{5,4},{6,7},{7,6},{8,9},{9,8},{10,11... | collective-permute-start | bytes 3145736 | tf_op jit(solution)/shard_map/ppermute | solution.py:18
  2.3 5.8 %copy-start = (bf16[1,4096,2048]{2,1,0:T(8,128)(2,1)S(1)}, bf16[1,4096,2048]{2,1,0:T(8,128)(2,1)}, u32[]{:S(2)}) copy-start(bf16[1,4096,2048]{2,1,0:T(8,128)(2,1)} %param.5) | copy-start | bytes 50331652
  8.1 1.7 %copy-start.2 = (bf16[1,256,2048]{2,1,0:T(8,128)(2,1)S(1)}, bf16[1,256,2048]{2,1,0:T(8,128)(2,1)}, u32[]{:S(2)}) copy-start(bf16[1,256,2048]{2,1,0:T(8,128)(2,1)} %param.4) | copy-start | bytes 3145732
  8.1 18.9 %copy-start.3 = (bf16[1,256,2048]{2,1,0:T(8,128)(2,1)S(1)}, bf16[1,256,2048]{2,1,0:T(8,128)(2,1)}, u32[]{:S(2)}) copy-start(bf16[1,256,2048]{2,1,0:T(8,128)(2,1)} %param.6) | copy-start | bytes 3145732
  9.8 23.8 %copy-start.1 = (bf16[1,256,2048]{2,1,0:T(8,128)(2,1)S(1)}, bf16[1,256,2048]{2,1,0:T(8,128)(2,1)}, u32[]{:S(2)}) copy-start(bf16[1,256,2048]{2,1,0:T(8,128)(2,1)} %param.7) | copy-start | bytes 3145732
  9.8 38.5 %collective-permute-start.4 = (bf16[256,2048]{1,0:T(8,128)(2,1)S(1)}, bf16[256,2048]{1,0:T(8,128)(2,1)S(1)}, u32[]{:S(2)}, u32[]{:S(2)}) collective-permute-start(bf16[256,2048]{1,0:T(8,128)(2,1)S(1)} %bitcast.13), channel_id=1, source_target_pairs={{0,1},{1,0},{2,3},{3,2},{4,5},{5,4},{6,7},{7,6},{8,9},{9,8},{10,11... | collective-permute-start | bytes 3145736 | tf_op jit(solution)/shard_map/ppermute | solution.py:18
  29.0 19.3 %collective-permute-start.1 = (bf16[128,1024]{1,0:T(8,128)(2,1)S(1)}, bf16[128,1024]{1,0:T(8,128)(2,1)S(1)}, u32[]{:S(2)}, u32[]{:S(2)}) collective-permute-start(bf16[128,1024]{1,0:T(8,128)(2,1)S(1)} %get-tuple-element.28), channel_id=1, source_target_pairs={{0,8},{8,16},{16,24},{24,0},{1,9},{9,17},{17,25},{25,1},{2,10},{10... | collective-permute-start | bytes 786440 | tf_op jit(solution)/shard_map/ppermute | solution.py:18
  30.6 20.4 %collective-permute-start.2 = (bf16[128,1024]{1,0:T(8,128)(2,1)S(1)}, bf16[128,1024]{1,0:T(8,128)(2,1)S(1)}, u32[]{:S(2)}, u32[]{:S(2)}) collective-permute-start(bf16[128,1024]{1,0:T(8,128)(2,1)S(1)} %get-tuple-element.29), channel_id=1, source_target_pairs={{0,16},{8,24},{16,0},{24,8},{1,17},{9,25},{17,1},{25,9},{2,18},{10... | collective-permute-start | bytes 786440 | tf_op jit(solution)/shard_map/ppermute | solution.py:18
  31.7 21.1 %collective-permute-start.3 = (bf16[128,1024]{1,0:T(8,128)(2,1)S(1)}, bf16[128,1024]{1,0:T(8,128)(2,1)S(1)}, u32[]{:S(2)}, u32[]{:S(2)}) collective-permute-start(bf16[128,1024]{1,0:T(8,128)(2,1)S(1)} %get-tuple-element.30), channel_id=1, source_target_pairs={{0,24},{8,0},{16,8},{24,16},{1,25},{9,1},{17,9},{25,17},{2,26},{10... | collective-permute-start | bytes 786440 | tf_op jit(solution)/shard_map/ppermute | solution.py:18
  52.8 26.5 %collective-permute-start.5 = (bf16[256,2176]{1,0:T(8,128)(2,1)S(1)}, bf16[256,2176]{1,0:T(8,128)(2,1)S(1)}, u32[]{:S(2)}, u32[]{:S(2)}) collective-permute-start(bf16[256,2176]{1,0:T(8,128)(2,1)S(1)} %get-tuple-element.34), channel_id=1, source_target_pairs={{0,1},{1,0},{2,3},{3,2},{4,5},{5,4},{6,7},{7,6},{8,9},{9,8},{10,11... | collective-permute-start | bytes 3342344 | tf_op jit(solution)/shard_map/ppermute | solution.py:18
  54.3 27.5 %collective-permute-start.10 = (bf16[256,2048]{1,0:T(8,128)(2,1)S(1)}, bf16[256,2048]{1,0:T(8,128)(2,1)S(1)}, u32[]{:S(2)}, u32[]{:S(2)}) collective-permute-start(bf16[256,2048]{1,0:T(8,128)(2,1)S(1)} %get-tuple-element.39.refs_0_), channel_id=1, source_target_pairs={{8,0},{16,8},{24,16},{9,1},{17,9},{25,17},{10,2},{18,10},{26,18},{... | collective-permute-start | bytes 3145736 | tf_op jit(solution)/shard_map/ppermute | solution.py:29
  56.2 26.7 %collective-permute-start.8 = (bf16[256,2048]{1,0:T(8,128)(2,1)S(1)}, bf16[256,2048]{1,0:T(8,128)(2,1)S(1)}, u32[]{:S(2)}, u32[]{:S(2)}) collective-permute-start(bf16[256,2048]{1,0:T(8,128)(2,1)S(1)} %get-tuple-element.39.refs_0_), channel_id=1, source_target_pairs={{0,8},{8,16},{16,24},{1,9},{9,17},{17,25},{2,10},{10,18},{18,26},{... | collective-permute-start | bytes 3145736 | tf_op jit(solution)/shard_map/ppermute | solution.py:29
  79.3 23.8 %collective-permute-start.6 = (bf16[256,2048]{1,0:T(8,128)(2,1)S(1)}, bf16[256,2048]{1,0:T(8,128)(2,1)S(1)}, u32[]{:S(2)}, u32[]{:S(2)}) collective-permute-start(bf16[256,2048]{1,0:T(8,128)(2,1)S(1)} %forward_layer.2), channel_id=1, source_target_pairs={{0,3},{1,2},{2,5},{3,4},{4,7},{5,6},{6,1},{7,0},{8,11},{9,10},{10,... | collective-permute-start | bytes 3145736 | tf_op jit(solution)/shard_map/ppermute | solution.py:45
  79.5 26.4 %collective-permute-start.13 = (bf16[256,2048]{1,0:T(8,128)(2,1)S(1)}, bf16[256,2048]{1,0:T(8,128)(2,1)S(1)}, u32[]{:S(2)}, u32[]{:S(2)}) collective-permute-start(bf16[256,2048]{1,0:T(8,128)(2,1)S(1)} %forward_layer.2), channel_id=1, source_target_pairs={{0,2},{2,4},{4,6},{6,0},{1,3},{3,5},{5,7},{7,1},{8,10},{10,12},{12... | collective-permute-start | bytes 3145736 | tf_op jit(solution)/shard_map/ppermute | solution.py:18
  82.9 30.4 %collective-permute-start.11 = (bf16[256,2048]{1,0:T(8,128)(2,1)S(1)}, bf16[256,2048]{1,0:T(8,128)(2,1)S(1)}, u32[]{:S(2)}, u32[]{:S(2)}) collective-permute-start(bf16[256,2048]{1,0:T(8,128)(2,1)S(1)} %get-tuple-element.39.refs_0_), channel_id=1, source_target_pairs={{0,24},{24,0},{1,25},{25,1},{2,26},{26,2},{3,27},{27,3},{4,28},{28... | collective-permute-start | bytes 3145736 | tf_op jit(solution)/shard_map/ppermute | solution.py:35
  83.6 47.4 %collective-permute-start.12 = (bf16[256,2048]{1,0:T(8,128)(2,1)S(1)}, bf16[256,2048]{1,0:T(8,128)(2,1)S(1)}, u32[]{:S(2)}, u32[]{:S(2)}) collective-permute-start(bf16[256,2048]{1,0:T(8,128)(2,1)S(1)} %collective-permute-done.10.refs_6_), channel_id=1, source_target_pairs={{8,0},{16,8},{9,1},{17,9},{10,2},{18,10},{11,3},{19,11},{12,4},{20... | collective-permute-start | bytes 3145736 | tf_op jit(solution)/shard_map/ppermute | solution.py:29
  89.6 41.4 %collective-permute-start.9 = (bf16[256,2048]{1,0:T(8,128)(2,1)S(1)}, bf16[256,2048]{1,0:T(8,128)(2,1)S(1)}, u32[]{:S(2)}, u32[]{:S(2)}) collective-permute-start(bf16[256,2048]{1,0:T(8,128)(2,1)S(1)} %collective-permute-done.8.refs_1_), channel_id=1, source_target_pairs={{8,16},{16,24},{9,17},{17,25},{10,18},{18,26},{11,19},{19,27},{12,... | collective-permute-start | bytes 3145736 | tf_op jit(solution)/shard_map/ppermute | solution.py:29
  103.1 31.5 %collective-permute-start.15 = (bf16[256,2048]{1,0:T(8,128)(2,1)S(1)}, bf16[256,2048]{1,0:T(8,128)(2,1)S(1)}, u32[]{:S(2)}, u32[]{:S(2)}) collective-permute-start(bf16[256,2048]{1,0:T(8,128)(2,1)S(1)} %input_grads.1), channel_id=1, source_target_pairs={{0,6},{2,0},{4,2},{6,4},{1,7},{3,1},{5,3},{7,5},{8,14},{10,8},{12,... | collective-permute-start | bytes 3145736 | tf_op jit(solution)/shard_map/ppermute | solution.py:18
  113.2 21.4 %collective-permute-start.14 = (bf16[256,2048]{1,0:T(8,128)(2,1)S(1)}, bf16[256,2048]{1,0:T(8,128)(2,1)S(1)}, u32[]{:S(2)}, u32[]{:S(2)}) collective-permute-start(bf16[256,2048]{1,0:T(8,128)(2,1)S(1)} %forward_layer.3), channel_id=1, source_target_pairs={{0,6},{2,0},{4,2},{6,4},{1,7},{3,1},{5,3},{7,5},{8,14},{10,8},{12,... | collective-permute-start | bytes 3145736 | tf_op jit(solution)/shard_map/ppermute | solution.py:18
  113.3 20.0 %collective-permute-start.7 = (bf16[384,1024]{1,0:T(8,128)(2,1)S(1)}, bf16[384,1024]{1,0:T(8,128)(2,1)S(1)}, u32[]{:S(2)}, u32[]{:S(2)}) collective-permute-start(bf16[384,1024]{1,0:T(8,128)(2,1)S(1)} %stack_blocks.1), channel_id=1, source_target_pairs={{0,1},{1,0},{2,3},{3,2},{4,5},{5,4},{6,7},{7,6},{8,9},{9,8},{10,11... | collective-permute-start | bytes 2359304 | tf_op jit(solution)/shard_map/ppermute | solution.py:18

commit v4 on v3

--- a/solution.py
+++ b/solution.py
@@ -353,7 +353,7 @@
             ups.append(along(ups[-1], "dp", 1, steps - 1))
             downs.append(along(downs[-1], "dp", -1, steps - 1))
         else:
-            ups.append(across(after(grad, ups[1], downs[1]), "dp", steps))
+            ups.append(across(grad, "dp", steps))
             downs.append(ups[-1])
 
     forward = forward_layer(place, own_in, other_in, weight)

time: 142 us -> 141 us (level)
    ppermute x4, waiting for transfers between devices: 18 us -> 14.1 us  [along(): return lax.ppermute(value, axis, pairs)]
    ppermute x10, waiting for transfers between devices: 38.6 us -> 41.4 us  [shift(): lax.ppermute(value, axis, [(at, (at + steps) % count) for at in range(cou...]
    ppermute x1, waiting for transfers between devices: 10.1 us -> 12.6 us  [shift_and_swap(): return lax.ppermute(value, ('section', 'mp'), pairs)]
where the time goes in v4:
time: 141 us
  waiting for transfers between devices  68.1 us (48%)
  Pallas kernels  38.5 us (27%)
  starting transfers between devices  27.3 us (19%)
  local copies, waits for them, and re-layouts  5.78 us (4%)
    ppermute x10, waiting for transfers between devices, shift(): lax.ppermute(value, axis, [(at, (at + steps) % count) for at in range(cou...  41.4 us
    pallas_call x8, Pallas kernels, call(): pl.pallas_call(run, in_specs=[SMEM] + [VMEM] * len(values) + [ANY] * len(...  30.7 us
    ppermute x10, starting transfers between devices, shift(): lax.ppermute(value, axis, [(at, (at + steps) % count) for at in range(cou...  14.4 us
    ppermute x4, waiting for transfers between devices, along(): return lax.ppermute(value, axis, pairs)  14.1 us
    ppermute x1, waiting for transfers between devices, shift_and_swap(): return lax.ppermute(value, ('section', 'mp'), pairs)  12.6 us
    ppermute x4, starting transfers between devices, along(): return lax.ppermute(value, axis, pairs)  12 us
    pallas_call x1, Pallas kernels, weight_grads(): pl.pallas_call(functools.partial(weight_grad_kernel, len(passes), width=w...  6.08 us
    unnamed x8, local copies, waits for them, and re-layouts  5.78 us
  transfers between devices with their start and end apart: 16, of which 9 were waited for; matrix products, arithmetic and copies ran while one was open for 0% of the time, Pallas kernels for 23%

profile of v4, /device:TPU:8, one launch (start us, length us, event | category | flops | bytes accessed | tf_op | source)
XLA Modules:
  0.0 140.8 jit_solution(1757464586041964611)
XLA Ops:
  0.6 1.6 %collective-permute-start = (bf16[256,2048]{1,0:T(8,128)(2,1)}, bf16[256,2048]{1,0:T(8,128)(2,1)S(1)}, u32[]{:S(2)}, u32[]{:S(2)}) collective-permute-start(bf16[256,2048]{1,0:T(8,128)(2,1)} %bitcast.15), channel_id=1, source_target_pairs={{0,1},{1,0},{2,3},{3,2},{4,5},{5,4},{6,7},{7,6},{8,9},{9,8},{10,11... | collective-permute-start | bytes 3145736 | tf_op jit(solution)/shard_map/ppermute | solution.py:18
  2.3 5.8 %copy-done = bf16[1,4096,2048]{2,1,0:T(8,128)(2,1)S(1)} copy-done((bf16[1,4096,2048]{2,1,0:T(8,128)(2,1)S(1)}, bf16[1,4096,2048]{2,1,0:T(8,128)(2,1)}, u32[]{:S(2)}) %copy-start) | copy-done | bytes 16777240
  8.1 1.7 %load_weights.1.refs_2_.refs_1_ = bf16[4096,2048]{1,0:T(8,128)(2,1)S(1)} custom-call(s32[2]{0:T(128)S(1)} %pad_add_fusion.place_ref, bf16[4096,2048]{1,0:T(8,128)(2,1)S(1)} %bitcast.10), custom_call_target="tpu_custom_call" | custom-call | tf_op jit(solution)/shard_map/load_weights/pallas_call | solution.py:196
  10.4 16.6 %collective-permute-done.refs_1_ = bf16[256,2048]{1,0:T(8,128)(2,1)S(1)} collective-permute-done((bf16[256,2048]{1,0:T(8,128)(2,1)}, bf16[256,2048]{1,0:T(8,128)(2,1)S(1)}, u32[]{:S(2)}, u32[]{:S(2)}) %collective-permute-start) | collective-permute-done | bytes 1048608 | tf_op jit(solution)/shard_map/ppermute | solution.py:18
  27.0 2.0 %norm_rows.1 = (bf16[256,4096]{1,0:T(8,128)(2,1)S(1)}, f32[256,128]{1,0:T(8,128)S(1)}, bf16[256,2048]{1,0:T(8,128)(2,1)S(1)}, bf16[256,1024]{1,0:T(8,128)(2,1)S(...) custom-call(s32[2]{0:T(128)S(1)} %pad_add_fusion.place_ref, ...), custom_call_target="tpu_custom_call" | custom-call | flops 1000 | bytes 1000 | tf_op jit(solution)/shard_map/norm_rows/pallas_call | solution.py:59
  29.0 1.6 %collective-permute-start.1 = (bf16[128,1024]{1,0:T(8,128)(2,1)S(1)}, bf16[128,1024]{1,0:T(8,128)(2,1)S(1)}, u32[]{:S(2)}, u32[]{:S(2)}) collective-permute-start(bf16[128,1024]{1,0:T(8,128)(2,1)S(1)} %get-tuple-element.27), channel_id=1, source_target_pairs={{0,8},{8,16},{16,24},{24,0},{1,9},{9,17},{17,25},{25,1},{2,10},{10... | collective-permute-start | bytes 786440 | tf_op jit(solution)/shard_map/ppermute | solution.py:18
  31.7 1.9 %collective-permute-start.3 = (bf16[128,1024]{1,0:T(8,128)(2,1)S(1)}, bf16[128,1024]{1,0:T(8,128)(2,1)S(1)}, u32[]{:S(2)}, u32[]{:S(2)}) collective-permute-start(bf16[128,1024]{1,0:T(8,128)(2,1)S(1)} %get-tuple-element.29), channel_id=1, source_target_pairs={{0,24},{8,0},{16,8},{24,16},{1,25},{9,1},{17,9},{25,17},{2,26},{10... | collective-permute-start | bytes 786440 | tf_op jit(solution)/shard_map/ppermute | solution.py:18
  33.6 10.2 %backward_rows.1 = (bf16[256,2048]{1,0:T(8,128)(2,1)S(1)}, bf16[256,2176]{1,0:T(8,128)(2,1)S(1)}, f32[256,2048]{1,0:T(8,128)S(1)}, f32[256,128]{1,0:T(8,128)S(1)}) custom-call(s32[2]{0:T(128)S(1)} %pad_add_fusion.place_ref, bf16[256,4096]{1,0:T(8,128)(2,1)S(1)} %get-tuple-element.31.refs_0_, bf16[4096,2048]{1,0:T(8,128)(2,1)S(1)} %load_weights.1.refs_2_.refs_1_, ...), custom_call_target="tpu_custom_call" | custom-call | flops 1000 | bytes 1000 | tf_op jit(solution)/shard_map/backward_rows/pallas_call | solution.py:59
  43.8 4.5 %collective-permute-done.4.refs_1_ = bf16[256,2048]{1,0:T(8,128)(2,1)S(1)} collective-permute-done((bf16[256,2048]{1,0:T(8,128)(2,1)S(1)}, bf16[256,2048]{1,0:T(8,128)(2,1)S(1)}, u32[]{:S(2)}, u32[]{:S(2)}) %collective-permute-start.4) | collective-permute-done | bytes 1048608 | tf_op jit(solution)/shard_map/ppermute | solution.py:18
  48.3 2.7 %collective-permute-done.2.refs_1_.refs_2_ = bf16[128,1024]{1,0:T(8,128)(2,1)S(1)} collective-permute-done((bf16[128,1024]{1,0:T(8,128)(2,1)S(1)}, bf16[128,1024]{1,0:T(8,128)(2,1)S(1)}, u32[]{:S(2)}, u32[]{:S(2)}) %collective-permute-start.2) | collective-permute-done | bytes 262176 | tf_op jit(solution)/shard_map/ppermute | solution.py:18
  51.0 1.8 %collective-permute-done.3.refs_2_.refs_3_ = bf16[128,1024]{1,0:T(8,128)(2,1)S(1)} collective-permute-done((bf16[128,1024]{1,0:T(8,128)(2,1)S(1)}, bf16[128,1024]{1,0:T(8,128)(2,1)S(1)}, u32[]{:S(2)}, u32[]{:S(2)}) %collective-permute-start.3) | collective-permute-done | bytes 262176 | tf_op jit(solution)/shard_map/ppermute | solution.py:18
  54.3 1.9 %collective-permute-start.11 = (bf16[256,2048]{1,0:T(8,128)(2,1)S(1)}, bf16[256,2048]{1,0:T(8,128)(2,1)S(1)}, u32[]{:S(2)}, u32[]{:S(2)}) collective-permute-start(bf16[256,2048]{1,0:T(8,128)(2,1)S(1)} %get-tuple-element.37.refs_0_), channel_id=1, source_target_pairs={{8,0},{16,8},{24,16},{9,1},{17,9},{25,17},{10,2},{18,10},{26,18},{... | collective-permute-start | bytes 3145736 | tf_op jit(solution)/shard_map/ppermute | solution.py:29
  56.2 4.1 %collective-permute-start.8 = (bf16[256,2048]{1,0:T(8,128)(2,1)S(1)}, bf16[256,2048]{1,0:T(8,128)(2,1)S(1)}, u32[]{:S(2)}, u32[]{:S(2)}) collective-permute-start(bf16[256,2048]{1,0:T(8,128)(2,1)S(1)} %get-tuple-element.37.refs_0_), channel_id=1, source_target_pairs={{0,8},{8,16},{16,24},{1,9},{9,17},{17,25},{2,10},{10,18},{18,26},{... | collective-permute-start | bytes 3145736 | tf_op jit(solution)/shard_map/ppermute | solution.py:29
  60.3 7.2 %forward_layer.2 = bf16[256,2048]{1,0:T(8,128)(2,1)S(1)} custom-call(s32[2]{0:T(128)S(1)} %pad_add_fusion.place_ref, bf16[256,2048]{1,0:T(8,128)(2,1)S(1)} %bitcast.14, bf16[256,2048]{1,0:T(8,128)(2,1)S(1)} %collective-permute-done.4.refs_1_, bf16[4096,2048]{1,0:T(8,128)(2,1)S(1)} %load_weights.1.refs_2_.refs_1_), custom_call_target="tpu_custom_call" | custom-call | flops 1000 | bytes 1000 | tf_op jit(solution)/shard_map/forward_layer/pallas_call | solution.py:59
  67.5 11.8 %collective-permute-done.5.refs_2_ = bf16[256,2176]{1,0:T(8,128)(2,1)S(1)} collective-permute-done((bf16[256,2176]{1,0:T(8,128)(2,1)S(1)}, bf16[256,2176]{1,0:T(8,128)(2,1)S(1)}, u32[]{:S(2)}, u32[]{:S(2)}) %collective-permute-start.5) | collective-permute-done | bytes 1114144 | tf_op jit(solution)/shard_map/ppermute | solution.py:18
  79.5 2.3 %collective-permute-start.13 = (bf16[256,2048]{1,0:T(8,128)(2,1)S(1)}, bf16[256,2048]{1,0:T(8,128)(2,1)S(1)}, u32[]{:S(2)}, u32[]{:S(2)}) collective-permute-start(bf16[256,2048]{1,0:T(8,128)(2,1)S(1)} %forward_layer.2), channel_id=1, source_target_pairs={{0,2},{2,4},{4,6},{6,0},{1,3},{3,5},{5,7},{7,1},{8,10},{10,12},{12... | collective-permute-start | bytes 3145736 | tf_op jit(solution)/shard_map/ppermute | solution.py:18
  82.5 3.1 %collective-permute-start.12 = (bf16[256,2048]{1,0:T(8,128)(2,1)S(1)}, bf16[256,2048]{1,0:T(8,128)(2,1)S(1)}, u32[]{:S(2)}, u32[]{:S(2)}) collective-permute-start(bf16[256,2048]{1,0:T(8,128)(2,1)S(1)} %collective-permute-done.11.refs_6_), channel_id=1, source_target_pairs={{8,0},{16,8},{9,1},{17,9},{10,2},{18,10},{11,3},{19,11},{12,4},{20... | collective-permute-start | bytes 3145736 | tf_op jit(solution)/shard_map/ppermute | solution.py:29
  85.7 2.8 %collective-permute-start.9 = (bf16[256,2048]{1,0:T(8,128)(2,1)S(1)}, bf16[256,2048]{1,0:T(8,128)(2,1)S(1)}, u32[]{:S(2)}, u32[]{:S(2)}) collective-permute-start(bf16[256,2048]{1,0:T(8,128)(2,1)S(1)} %collective-permute-done.8.refs_1_), channel_id=1, source_target_pairs={{8,16},{16,24},{9,17},{17,25},{10,18},{18,26},{11,19},{19,27},{12,... | collective-permute-start | bytes 3145736 | tf_op jit(solution)/shard_map/ppermute | solution.py:29
  90.5 12.6 %collective-permute-done.6.refs_1_ = bf16[256,2048]{1,0:T(8,128)(2,1)S(1)} collective-permute-done((bf16[256,2048]{1,0:T(8,128)(2,1)S(1)}, bf16[256,2048]{1,0:T(8,128)(2,1)S(1)}, u32[]{:S(2)}, u32[]{:S(2)}) %collective-permute-start.6) | collective-permute-done | bytes 1048608 | tf_op jit(solution)/shard_map/ppermute | solution.py:45
  103.1 2.9 %collective-permute-start.15 = (bf16[256,2048]{1,0:T(8,128)(2,1)S(1)}, bf16[256,2048]{1,0:T(8,128)(2,1)S(1)}, u32[]{:S(2)}, u32[]{:S(2)}) collective-permute-start(bf16[256,2048]{1,0:T(8,128)(2,1)S(1)} %input_grads.1), channel_id=1, source_target_pairs={{0,6},{2,0},{4,2},{6,4},{1,7},{3,1},{5,3},{7,5},{8,14},{10,8},{12,... | collective-permute-start | bytes 3145736 | tf_op jit(solution)/shard_map/ppermute | solution.py:18
  106.0 7.2 %forward_layer.3 = bf16[256,2048]{1,0:T(8,128)(2,1)S(1)} custom-call(s32[2]{0:T(128)S(1)} %pad_add_fusion.place_ref, bf16[256,2048]{1,0:T(8,128)(2,1)S(1)} %collective-permute-done.13.refs_0_.refs_2_, bf16[256,2048]{1,0:T(8,128)(2,1)S(1)} %collective-permute-done.6.refs_1_, bf16[4096,2048]{1,0:T(8,128)(2,1)S(1)} %load_weights.1.refs_2_.refs_1_), custom_call_target="tpu_custom_call" | custom-call | flops 1000 | bytes 1000 | tf_op jit(solution)/shard_map/forward_layer/pallas_call | solution.py:59
  114.1 13.9 %collective-permute-done.12.refs_5_ = bf16[256,2048]{1,0:T(8,128)(2,1)S(1)} collective-permute-done((bf16[256,2048]{1,0:T(8,128)(2,1)S(1)}, bf16[256,2048]{1,0:T(8,128)(2,1)S(1)}, u32[]{:S(2)}, u32[]{:S(2)}) %collective-permute-start.12) | collective-permute-done | bytes 1048608 | tf_op jit(solution)/shard_map/ppermute | solution.py:29
  129.1 4.1 %collective-permute-done.7.refs_4_ = bf16[384,1024]{1,0:T(8,128)(2,1)S(1)} collective-permute-done((bf16[384,1024]{1,0:T(8,128)(2,1)S(1)}, bf16[384,1024]{1,0:T(8,128)(2,1)S(1)}, u32[]{:S(2)}, u32[]{:S(2)}) %collective-permute-start.7) | collective-permute-done | bytes 786464 | tf_op jit(solution)/shard_map/ppermute | solution.py:18
  134.6 6.1 %weight_grads.1 = (bf16[1024,2048]{1,0:T(8,128)(2,1)}, bf16[256,2048]{1,0:T(8,128)(2,1)}, bf16[256,2048]{1,0:T(8,128)(2,1)}, bf16[256,2048]{1,0:T(8,128)(2,1)}) custom-call(s32[2]{0:T(128)S(1)} %pad_add_fusion.place_ref, bf16[1024,1024]{1,0:T(8,128)(2,1)S(1)} %gather_blocks.1.refs_0_, bf16[1024,2048]{1,0:T(8,128)(2,1)S(1)} %gather_grads.1.refs_1_, ...), custom_call_target="tpu_custom_call" | custom-call | flops 1000 | bytes 1000 | tf_op jit(solution)/shard_map/weight_grads/pallas_call | solution.py:312
  (27 shorter events, 9.5 us)
Async XLA Ops:
  0.6 26.3 %collective-permute-start = (bf16[256,2048]{1,0:T(8,128)(2,1)}, bf16[256,2048]{1,0:T(8,128)(2,1)S(1)}, u32[]{:S(2)}, u32[]{:S(2)}) collective-permute-start(bf16[256,2048]{1,0:T(8,128)(2,1)} %bitcast.15), channel_id=1, source_target_pairs={{0,1},{1,0},{2,3},{3,2},{4,5},{5,4},{6,7},{7,6},{8,9},{9,8},{10,11... | collective-permute-start | bytes 3145736 | tf_op jit(solution)/shard_map/ppermute | solution.py:18
  2.3 5.8 %copy-start = (bf16[1,4096,2048]{2,1,0:T(8,128)(2,1)S(1)}, bf16[1,4096,2048]{2,1,0:T(8,128)(2,1)}, u32[]{:S(2)}) copy-start(bf16[1,4096,2048]{2,1,0:T(8,128)(2,1)} %param.5) | copy-start | bytes 50331652
  8.1 1.7 %copy-start.2 = (bf16[1,256,2048]{2,1,0:T(8,128)(2,1)S(1)}, bf16[1,256,2048]{2,1,0:T(8,128)(2,1)}, u32[]{:S(2)}) copy-start(bf16[1,256,2048]{2,1,0:T(8,128)(2,1)} %param.4) | copy-start | bytes 3145732
  8.1 18.9 %copy-start.3 = (bf16[1,256,2048]{2,1,0:T(8,128)(2,1)S(1)}, bf16[1,256,2048]{2,1,0:T(8,128)(2,1)}, u32[]{:S(2)}) copy-start(bf16[1,256,2048]{2,1,0:T(8,128)(2,1)} %param.6) | copy-start | bytes 3145732
  9.8 23.8 %copy-start.1 = (bf16[1,256,2048]{2,1,0:T(8,128)(2,1)S(1)}, bf16[1,256,2048]{2,1,0:T(8,128)(2,1)}, u32[]{:S(2)}) copy-start(bf16[1,256,2048]{2,1,0:T(8,128)(2,1)} %param.7) | copy-start | bytes 3145732
  9.8 38.5 %collective-permute-start.4 = (bf16[256,2048]{1,0:T(8,128)(2,1)S(1)}, bf16[256,2048]{1,0:T(8,128)(2,1)S(1)}, u32[]{:S(2)}, u32[]{:S(2)}) collective-permute-start(bf16[256,2048]{1,0:T(8,128)(2,1)S(1)} %bitcast.13), channel_id=1, source_target_pairs={{0,1},{1,0},{2,3},{3,2},{4,5},{5,4},{6,7},{7,6},{8,9},{9,8},{10,11... | collective-permute-start | bytes 3145736 | tf_op jit(solution)/shard_map/ppermute | solution.py:18
  29.0 19.3 %collective-permute-start.1 = (bf16[128,1024]{1,0:T(8,128)(2,1)S(1)}, bf16[128,1024]{1,0:T(8,128)(2,1)S(1)}, u32[]{:S(2)}, u32[]{:S(2)}) collective-permute-start(bf16[128,1024]{1,0:T(8,128)(2,1)S(1)} %get-tuple-element.27), channel_id=1, source_target_pairs={{0,8},{8,16},{16,24},{24,0},{1,9},{9,17},{17,25},{25,1},{2,10},{10... | collective-permute-start | bytes 786440 | tf_op jit(solution)/shard_map/ppermute | solution.py:18
  30.6 20.4 %collective-permute-start.2 = (bf16[128,1024]{1,0:T(8,128)(2,1)S(1)}, bf16[128,1024]{1,0:T(8,128)(2,1)S(1)}, u32[]{:S(2)}, u32[]{:S(2)}) collective-permute-start(bf16[128,1024]{1,0:T(8,128)(2,1)S(1)} %get-tuple-element.28), channel_id=1, source_target_pairs={{0,16},{8,24},{16,0},{24,8},{1,17},{9,25},{17,1},{25,9},{2,18},{10... | collective-permute-start | bytes 786440 | tf_op jit(solution)/shard_map/ppermute | solution.py:18
  31.7 21.1 %collective-permute-start.3 = (bf16[128,1024]{1,0:T(8,128)(2,1)S(1)}, bf16[128,1024]{1,0:T(8,128)(2,1)S(1)}, u32[]{:S(2)}, u32[]{:S(2)}) collective-permute-start(bf16[128,1024]{1,0:T(8,128)(2,1)S(1)} %get-tuple-element.29), channel_id=1, source_target_pairs={{0,24},{8,0},{16,8},{24,16},{1,25},{9,1},{17,9},{25,17},{2,26},{10... | collective-permute-start | bytes 786440 | tf_op jit(solution)/shard_map/ppermute | solution.py:18
  52.8 26.5 %collective-permute-start.5 = (bf16[256,2176]{1,0:T(8,128)(2,1)S(1)}, bf16[256,2176]{1,0:T(8,128)(2,1)S(1)}, u32[]{:S(2)}, u32[]{:S(2)}) collective-permute-start(bf16[256,2176]{1,0:T(8,128)(2,1)S(1)} %get-tuple-element.33), channel_id=1, source_target_pairs={{0,1},{1,0},{2,3},{3,2},{4,5},{5,4},{6,7},{7,6},{8,9},{9,8},{10,11... | collective-permute-start | bytes 3342344 | tf_op jit(solution)/shard_map/ppermute | solution.py:18
  54.3 28.3 %collective-permute-start.11 = (bf16[256,2048]{1,0:T(8,128)(2,1)S(1)}, bf16[256,2048]{1,0:T(8,128)(2,1)S(1)}, u32[]{:S(2)}, u32[]{:S(2)}) collective-permute-start(bf16[256,2048]{1,0:T(8,128)(2,1)S(1)} %get-tuple-element.37.refs_0_), channel_id=1, source_target_pairs={{8,0},{16,8},{24,16},{9,1},{17,9},{25,17},{10,2},{18,10},{26,18},{... | collective-permute-start | bytes 3145736 | tf_op jit(solution)/shard_map/ppermute | solution.py:29
  56.2 29.5 %collective-permute-start.8 = (bf16[256,2048]{1,0:T(8,128)(2,1)S(1)}, bf16[256,2048]{1,0:T(8,128)(2,1)S(1)}, u32[]{:S(2)}, u32[]{:S(2)}) collective-permute-start(bf16[256,2048]{1,0:T(8,128)(2,1)S(1)} %get-tuple-element.37.refs_0_), channel_id=1, source_target_pairs={{0,8},{8,16},{16,24},{1,9},{9,17},{17,25},{2,10},{10,18},{18,26},{... | collective-permute-start | bytes 3145736 | tf_op jit(solution)/shard_map/ppermute | solution.py:29
  79.3 23.8 %collective-permute-start.6 = (bf16[256,2048]{1,0:T(8,128)(2,1)S(1)}, bf16[256,2048]{1,0:T(8,128)(2,1)S(1)}, u32[]{:S(2)}, u32[]{:S(2)}) collective-permute-start(bf16[256,2048]{1,0:T(8,128)(2,1)S(1)} %forward_layer.2), channel_id=1, source_target_pairs={{0,3},{1,2},{2,5},{3,4},{4,7},{5,6},{6,1},{7,0},{8,11},{9,10},{10,... | collective-permute-start | bytes 3145736 | tf_op jit(solution)/shard_map/ppermute | solution.py:45
  79.5 26.4 %collective-permute-start.13 = (bf16[256,2048]{1,0:T(8,128)(2,1)S(1)}, bf16[256,2048]{1,0:T(8,128)(2,1)S(1)}, u32[]{:S(2)}, u32[]{:S(2)}) collective-permute-start(bf16[256,2048]{1,0:T(8,128)(2,1)S(1)} %forward_layer.2), channel_id=1, source_target_pairs={{0,2},{2,4},{4,6},{6,0},{1,3},{3,5},{5,7},{7,1},{8,10},{10,12},{12... | collective-permute-start | bytes 3145736 | tf_op jit(solution)/shard_map/ppermute | solution.py:18
  81.8 31.5 %collective-permute-start.10 = (bf16[256,2048]{1,0:T(8,128)(2,1)S(1)}, bf16[256,2048]{1,0:T(8,128)(2,1)S(1)}, u32[]{:S(2)}, u32[]{:S(2)}) collective-permute-start(bf16[256,2048]{1,0:T(8,128)(2,1)S(1)} %get-tuple-element.37.refs_0_), channel_id=1, source_target_pairs={{0,24},{24,0},{1,25},{25,1},{2,26},{26,2},{3,27},{27,3},{4,28},{28... | collective-permute-start | bytes 3145736 | tf_op jit(solution)/shard_map/ppermute | solution.py:35
  82.5 45.5 %collective-permute-start.12 = (bf16[256,2048]{1,0:T(8,128)(2,1)S(1)}, bf16[256,2048]{1,0:T(8,128)(2,1)S(1)}, u32[]{:S(2)}, u32[]{:S(2)}) collective-permute-start(bf16[256,2048]{1,0:T(8,128)(2,1)S(1)} %collective-permute-done.11.refs_6_), channel_id=1, source_target_pairs={{8,0},{16,8},{9,1},{17,9},{10,2},{18,10},{11,3},{19,11},{12,4},{20... | collective-permute-start | bytes 3145736 | tf_op jit(solution)/shard_map/ppermute | solution.py:29
  85.7 42.5 %collective-permute-start.9 = (bf16[256,2048]{1,0:T(8,128)(2,1)S(1)}, bf16[256,2048]{1,0:T(8,128)(2,1)S(1)}, u32[]{:S(2)}, u32[]{:S(2)}) collective-permute-start(bf16[256,2048]{1,0:T(8,128)(2,1)S(1)} %collective-permute-done.8.refs_1_), channel_id=1, source_target_pairs={{8,16},{16,24},{9,17},{17,25},{10,18},{18,26},{11,19},{19,27},{12,... | collective-permute-start | bytes 3145736 | tf_op jit(solution)/shard_map/ppermute | solution.py:29
  103.1 31.5 %collective-permute-start.15 = (bf16[256,2048]{1,0:T(8,128)(2,1)S(1)}, bf16[256,2048]{1,0:T(8,128)(2,1)S(1)}, u32[]{:S(2)}, u32[]{:S(2)}) collective-permute-start(bf16[256,2048]{1,0:T(8,128)(2,1)S(1)} %input_grads.1), channel_id=1, source_target_pairs={{0,6},{2,0},{4,2},{6,4},{1,7},{3,1},{5,3},{7,5},{8,14},{10,8},{12,... | collective-permute-start | bytes 3145736 | tf_op jit(solution)/shard_map/ppermute | solution.py:18
  113.2 21.4 %collective-permute-start.14 = (bf16[256,2048]{1,0:T(8,128)(2,1)S(1)}, bf16[256,2048]{1,0:T(8,128)(2,1)S(1)}, u32[]{:S(2)}, u32[]{:S(2)}) collective-permute-start(bf16[256,2048]{1,0:T(8,128)(2,1)S(1)} %forward_layer.3), channel_id=1, source_target_pairs={{0,6},{2,0},{4,2},{6,4},{1,7},{3,1},{5,3},{7,5},{8,14},{10,8},{12,... | collective-permute-start | bytes 3145736 | tf_op jit(solution)/shard_map/ppermute | solution.py:18
  113.3 20.0 %collective-permute-start.7 = (bf16[384,1024]{1,0:T(8,128)(2,1)S(1)}, bf16[384,1024]{1,0:T(8,128)(2,1)S(1)}, u32[]{:S(2)}, u32[]{:S(2)}) collective-permute-start(bf16[384,1024]{1,0:T(8,128)(2,1)S(1)} %stack_blocks.1), channel_id=1, source_target_pairs={{0,1},{1,0},{2,3},{3,2},{4,5},{5,4},{6,7},{7,6},{8,9},{9,8},{10,11... | collective-permute-start | bytes 2359304 | tf_op jit(solution)/shard_map/ppermute | solution.py:18
